TPU v7x, 32 devices: a whole 2x2x4 slice. The times are simulated.
32 devices in a mesh: row: 4 (over y, core), seq: 8 (over z, x).
Axes of the slice: x: 2, y: 2, z: 4, core: 2. Of those that a mesh axis runs over, the one named last changes fastest.
Arguments:
- inputs: bfloat16 [4, 1024, 2048], P('row', 'seq'), may hold values from -6 to 6
- lengths: int32 [4, 2], P('row'), may hold values from 352 to 672, as said below
- w_query: bfloat16 [2048, 2048], P(('row', 'seq')), may hold values from -0.1875 to 0.1875
- w_key: bfloat16 [2048, 2048], P(('row', 'seq')), may hold values from -0.1875 to 0.1875
- w_value: bfloat16 [2048, 2048], P(('row', 'seq')), may hold values from -0.125 to 0.125
- w_out: bfloat16 [2048, 2048], P(('row', 'seq')), may hold values from -2.5 to 2.5
- gain_attn: bfloat16 [2048], P(('row', 'seq')), may hold values from 0.5 to 1.5
- w_gate: bfloat16 [2048, 8192], P(('row', 'seq')), may hold values from -0.125 to 0.125
- w_up: bfloat16 [2048, 8192], P(('row', 'seq')), may hold values from -0.125 to 0.125
- w_down: bfloat16 [8192, 2048], P(('row', 'seq')), may hold values from -0.0625 to 0.0625
- gain_mlp: bfloat16 [2048], P(('row', 'seq')), may hold values from 0.5 to 1.5
- cotangent: bfloat16 [4, 1024, 2048], P('row', 'seq'), may hold values from -6 to 6
Outputs:
- output: bfloat16 [4, 1024, 2048], P('row', 'seq')
- input_grad: float32 [4, 1024, 2048], P('row', 'seq')
- grad_query: float32 [2048, 2048], P(('row', 'seq'))
- grad_key: float32 [2048, 2048], P(('row', 'seq'))
- grad_value: float32 [2048, 2048], P(('row', 'seq'))
- grad_out: float32 [2048, 2048], P(('row', 'seq'))
- grad_gain_attn: float32 [2048], P(('row', 'seq'))
- grad_gate: float32 [2048, 8192], P(('row', 'seq'))
- grad_up: float32 [2048, 8192], P(('row', 'seq'))
- grad_down: float32 [8192, 2048], P(('row', 'seq'))
- grad_gain_mlp: float32 [2048], P(('row', 'seq'))
Inputs may be any that keep to these rules, and one draw needn't show every extreme that they name: The lengths of a row add up to 1024 and are multiples of 16.
All inputs are finite; a program needn't handle non-finite values.
Results may differ from a plain program's by a relative error of at most 0.012.
The roundings to bfloat16 on the way count: a program that leaves them out, or rounds other values in their place, can miss the bound.
Values may be sent and summed in bfloat16 or wider, within the bound.
A program may use at most 512 MiB of HBM per device.

v0:
```python
import jax
import jax.numpy as jnp
from jax import lax
from jax.sharding import PartitionSpec as P

HEADS = 16


EPSILON = 1e-05


def layout(lengths_row, places, block_rows, block_count):
    unit_counts = lengths_row // (2 * block_count)
    span_sizes = 2 * unit_counts
    offsets = jnp.cumsum(span_sizes) - span_sizes
    device = places // block_rows
    within_block = places - device * block_rows
    inside = (
        (within_block[:, None] >= offsets[None, :])
        & (within_block[:, None] < (offsets + span_sizes)[None, :])
    ).astype(jnp.int32)
    numbers = jnp.arange(lengths_row.shape[0], dtype=jnp.int32)
    segment = jnp.sum(inside * numbers[None, :], axis=1)
    unit_of = jnp.sum(inside * unit_counts[None, :], axis=1)
    begins = jnp.sum(inside * offsets[None, :], axis=1)
    length_of = jnp.sum(inside * lengths_row[None, :], axis=1)
    within = within_block - begins
    position = jnp.where(
        within < unit_of,
        device * unit_of + within,
        (2 * block_count - 1 - device) * unit_of + within - unit_of,
    )
    return (segment, position, length_of)


def rms_norm(values, gain):
    return values * lax.rsqrt(jnp.mean(values * values, axis=-1, keepdims=True) + EPSILON) * gain


def sigmoid_terms(query_heads, query_meta, key_heads, key_meta):
    query_segment, query_position, query_length = query_meta
    key_segment, key_position, unused_length = key_meta
    scores = jnp.einsum(
        "qhd,khd->hqk", query_heads, key_heads, preferred_element_type=jnp.float32
    ) * query_heads.shape[2] ** (-0.5)
    scores = scores - jnp.log(query_length.astype(jnp.float32))[None, :, None]
    allowed = (query_segment[:, None] == key_segment[None, :]) & (
        key_position[None, :] <= query_position[:, None]
    )
    return jnp.where(allowed[None], jax.nn.sigmoid(scores), 0.0)


def pair_terms(query_heads, query_meta, grad_heads, key_heads, key_meta, value_heads):
    sig_terms = sigmoid_terms(query_heads, query_meta, key_heads, key_meta)
    slopes = jnp.einsum("qhd,khd->hqk", grad_heads, value_heads, preferred_element_type=jnp.float32)
    score_grad = (slopes * sig_terms * (1.0 - sig_terms)).astype(jnp.bfloat16)
    return (sig_terms.astype(jnp.bfloat16), score_grad)


def by_blocks(step_fn, running, pieces, block_rows):
    size_total = pieces[0].shape[0]
    part_rows = 4 * block_rows
    block_count = size_total // part_rows

    def turn_over(step_number, carried):
        sub_pieces = tuple(
            (
                lax.dynamic_slice_in_dim(member, step_number * part_rows, part_rows, 0)
                for member in pieces
            )
        )
        return step_fn(carried, sub_pieces, step_number * part_rows)

    return lax.fori_loop(0, block_count, turn_over, running)


def local(
    inputs,
    lengths,
    w_query,
    w_key,
    w_value,
    w_out,
    gain_attn,
    w_gate,
    w_up,
    w_down,
    gain_mlp,
    cotangent,
):
    residual = inputs[0].astype(jnp.float32)
    tokens_here = residual.shape[0]
    model_width = residual.shape[1]
    head_size = model_width // HEADS
    score_scale = head_size ** (-0.5)
    block_total = lax.axis_size("seq")
    lengths_row = lengths[0]
    places = lax.axis_index("seq") * tokens_here + jnp.arange(tokens_here, dtype=jnp.int32)
    own_meta = layout(lengths_row, places, tokens_here, block_total)

    def meta_at(start_row, row_count):
        return layout(
            lengths_row,
            start_row + jnp.arange(row_count, dtype=jnp.int32),
            tokens_here,
            block_total,
        )

    def heads_of(matrix):
        return matrix.reshape(matrix.shape[0], HEADS, head_size)

    query_full, key_full, value_full, out_full, gain_one = (
        lax.all_gather(w_query, ("row", "seq"), axis=0, tiled=True),
        lax.all_gather(w_key, ("row", "seq"), axis=0, tiled=True),
        lax.all_gather(w_value, ("row", "seq"), axis=0, tiled=True),
        lax.all_gather(w_out, ("row", "seq"), axis=0, tiled=True),
        lax.all_gather(gain_attn, ("row", "seq"), axis=0, tiled=True),
    )
    gain_one_f = gain_one.astype(jnp.float32)
    normed = rms_norm(residual, gain_one_f).astype(jnp.bfloat16)
    queries = jnp.dot(normed, query_full, preferred_element_type=jnp.float32).astype(jnp.bfloat16)
    key_rows = jnp.dot(normed, key_full, preferred_element_type=jnp.float32).astype(jnp.bfloat16)
    value_rows = jnp.dot(normed, value_full, preferred_element_type=jnp.float32).astype(
        jnp.bfloat16
    )
    query_heads = heads_of(queries)

    def forward_step(running, pieces, start_row):
        key_piece, value_piece = pieces
        sig_terms = sigmoid_terms(
            query_heads, own_meta, heads_of(key_piece), meta_at(start_row, key_piece.shape[0])
        ).astype(jnp.bfloat16)
        added = jnp.einsum(
            "hqk,khd->qhd", sig_terms, heads_of(value_piece), preferred_element_type=jnp.float32
        )
        return running + added.reshape(tokens_here, model_width)

    attended = by_blocks(
        forward_step,
        jnp.zeros((tokens_here, model_width), jnp.float32),
        (
            lax.all_gather(key_rows, "seq", axis=0, tiled=True),
            lax.all_gather(value_rows, "seq", axis=0, tiled=True),
        ),
        tokens_here,
    )
    attended_low = attended.astype(jnp.bfloat16)
    middle = residual + jnp.dot(attended_low, out_full, preferred_element_type=jnp.float32)
    gate_full, up_full, down_full, gain_two = (
        lax.all_gather(w_gate, ("row", "seq"), axis=0, tiled=True),
        lax.all_gather(w_up, ("row", "seq"), axis=0, tiled=True),
        lax.all_gather(w_down, ("row", "seq"), axis=0, tiled=True),
        lax.all_gather(gain_mlp, ("row", "seq"), axis=0, tiled=True),
    )
    gain_two_f = gain_two.astype(jnp.float32)
    normed_mlp = rms_norm(middle, gain_two_f).astype(jnp.bfloat16)
    gate_vals = jnp.dot(normed_mlp, gate_full, preferred_element_type=jnp.float32)
    up_vals = jnp.dot(normed_mlp, up_full, preferred_element_type=jnp.float32)
    gated_prod, gated_back = jax.vjp(
        lambda gate_in, up_in: jax.nn.silu(gate_in) * up_in, gate_vals, up_vals
    )
    hidden = gated_prod.astype(jnp.bfloat16)
    output = (middle + jnp.dot(hidden, down_full, preferred_element_type=jnp.float32)).astype(
        jnp.bfloat16
    )
    upstream_low = cotangent[0]
    upstream = upstream_low.astype(jnp.float32)
    gate_full, up_full, down_full, gain_two = (
        lax.all_gather(w_gate, ("row", "seq"), axis=0, tiled=True),
        lax.all_gather(w_up, ("row", "seq"), axis=0, tiled=True),
        lax.all_gather(w_down, ("row", "seq"), axis=0, tiled=True),
        lax.all_gather(gain_mlp, ("row", "seq"), axis=0, tiled=True),
    )
    gain_two_f = gain_two.astype(jnp.float32)
    grad_down = jnp.dot(hidden.T, upstream_low, preferred_element_type=jnp.float32)
    shared_down = lax.psum_scatter(grad_down, ("row", "seq"), scatter_dimension=0, tiled=True)
    hidden_grad = jnp.dot(upstream_low, down_full.T, preferred_element_type=jnp.float32)
    gate_grad, up_grad = gated_back(hidden_grad)
    gate_low = gate_grad.astype(jnp.bfloat16)
    up_low = up_grad.astype(jnp.bfloat16)
    grad_gate = jnp.dot(normed_mlp.T, gate_low, preferred_element_type=jnp.float32)
    shared_gate = lax.psum_scatter(grad_gate, ("row", "seq"), scatter_dimension=0, tiled=True)
    normed_grad = jnp.dot(gate_low, gate_full.T, preferred_element_type=jnp.float32) + jnp.dot(
        up_low, up_full.T, preferred_element_type=jnp.float32
    )
    unused_mid, second_back = jax.vjp(rms_norm, middle, gain_two_f)
    middle_part, gain_two_grad = second_back(normed_grad)
    middle_grad = upstream + middle_part
    grad_up = jnp.dot(normed_mlp.T, up_low, preferred_element_type=jnp.float32)
    shared_up, shared_gain_two = (
        lax.psum_scatter(grad_up, ("row", "seq"), scatter_dimension=0, tiled=True),
        lax.psum_scatter(gain_two_grad, ("row", "seq"), scatter_dimension=0, tiled=True),
    )
    query_full, key_full, value_full, out_full, gain_one = (
        lax.all_gather(w_query, ("row", "seq"), axis=0, tiled=True),
        lax.all_gather(w_key, ("row", "seq"), axis=0, tiled=True),
        lax.all_gather(w_value, ("row", "seq"), axis=0, tiled=True),
        lax.all_gather(w_out, ("row", "seq"), axis=0, tiled=True),
        lax.all_gather(gain_attn, ("row", "seq"), axis=0, tiled=True),
    )
    gain_one_f = gain_one.astype(jnp.float32)
    branch_low = middle_grad.astype(jnp.bfloat16)
    grad_out = jnp.dot(attended_low.T, branch_low, preferred_element_type=jnp.float32)
    attended_grad = jnp.dot(branch_low, out_full.T, preferred_element_type=jnp.float32).astype(
        jnp.bfloat16
    )
    grad_heads = heads_of(attended_grad)
    key_heads_own = heads_of(key_rows)
    value_heads_own = heads_of(value_rows)

    def query_step(running, pieces, start_row):
        key_piece, value_piece = pieces
        key_piece_heads = heads_of(key_piece)
        unused_terms, score_grad = pair_terms(
            query_heads,
            own_meta,
            grad_heads,
            key_piece_heads,
            meta_at(start_row, key_piece.shape[0]),
            heads_of(value_piece),
        )
        added = jnp.einsum(
            "hqk,khd->qhd", score_grad, key_piece_heads, preferred_element_type=jnp.float32
        )
        return running + added.reshape(tokens_here, model_width) * score_scale

    start_value = jnp.zeros((tokens_here, model_width), jnp.float32)
    folded = by_blocks(
        query_step,
        start_value,
        (
            lax.all_gather(key_rows, "seq", axis=0, tiled=True),
            lax.all_gather(value_rows, "seq", axis=0, tiled=True),
        ),
        tokens_here,
    )

    def key_step(running, pieces, start_row):
        key_sum, value_sum = running
        query_piece, grad_piece = pieces
        row_count = query_piece.shape[0]
        query_piece_heads = heads_of(query_piece)
        grad_piece_heads = heads_of(grad_piece)
        sig_low, score_grad = pair_terms(
            query_piece_heads,
            meta_at(start_row, row_count),
            grad_piece_heads,
            key_heads_own,
            own_meta,
            value_heads_own,
        )
        key_add = jnp.einsum(
            "hqk,qhd->khd", score_grad, query_piece_heads, preferred_element_type=jnp.float32
        )
        value_add = jnp.einsum(
            "hqk,qhd->khd", sig_low, grad_piece_heads, preferred_element_type=jnp.float32
        )
        return (
            key_sum + key_add.reshape(tokens_here, model_width) * score_scale,
            value_sum + value_add.reshape(tokens_here, model_width),
        )

    empty_rows = jnp.zeros((tokens_here, model_width), jnp.float32)
    key_grad, value_grad = by_blocks(
        key_step,
        (empty_rows, empty_rows),
        (
            lax.all_gather(queries, "seq", axis=0, tiled=True),
            lax.all_gather(attended_grad, "seq", axis=0, tiled=True),
        ),
        tokens_here,
    )
    query_low = folded.astype(jnp.bfloat16)
    key_low = key_grad.astype(jnp.bfloat16)
    value_low = value_grad.astype(jnp.bfloat16)
    grad_query = jnp.dot(normed.T, query_low, preferred_element_type=jnp.float32)
    grad_key = jnp.dot(normed.T, key_low, preferred_element_type=jnp.float32)
    grad_value = jnp.dot(normed.T, value_low, preferred_element_type=jnp.float32)
    normed_back = jnp.dot(query_low, query_full.T, preferred_element_type=jnp.float32)
    normed_back = normed_back + jnp.dot(key_low, key_full.T, preferred_element_type=jnp.float32)
    normed_back = normed_back + jnp.dot(value_low, value_full.T, preferred_element_type=jnp.float32)
    unused_first, first_back = jax.vjp(rms_norm, residual, gain_one_f)
    residual_part, gain_one_grad = first_back(normed_back)
    input_grad = middle_grad + residual_part
    shared_query, shared_key, shared_value, shared_out, shared_gain_one = (
        lax.psum_scatter(grad_query, ("row", "seq"), scatter_dimension=0, tiled=True),
        lax.psum_scatter(grad_key, ("row", "seq"), scatter_dimension=0, tiled=True),
        lax.psum_scatter(grad_value, ("row", "seq"), scatter_dimension=0, tiled=True),
        lax.psum_scatter(grad_out, ("row", "seq"), scatter_dimension=0, tiled=True),
        lax.psum_scatter(gain_one_grad, ("row", "seq"), scatter_dimension=0, tiled=True),
    )
    return (
        output[None],
        input_grad[None],
        shared_query,
        shared_key,
        shared_value,
        shared_out,
        shared_gain_one,
        shared_gate,
        shared_up,
        shared_down,
        shared_gain_two,
    )


def solution(mesh):
    placed = (
        P("row", "seq", None),
        P("row", None),
        P(("row", "seq"), None),
        P(("row", "seq"), None),
        P(("row", "seq"), None),
        P(("row", "seq"), None),
        P(("row", "seq")),
        P(("row", "seq"), None),
        P(("row", "seq"), None),
        P(("row", "seq"), None),
        P(("row", "seq")),
        P("row", "seq", None),
    )
    return jax.shard_map(
        local,
        mesh=mesh,
        in_specs=placed,
        out_specs=(
            P("row", "seq", None),
            P("row", "seq", None),
            P(("row", "seq"), None),
            P(("row", "seq"), None),
            P(("row", "seq"), None),
            P(("row", "seq"), None),
            P(("row", "seq")),
            P(("row", "seq"), None),
            P(("row", "seq"), None),
            P(("row", "seq"), None),
            P(("row", "seq")),
        ),
        check_vma=False,
    )
```

profile of v0, /device:TPU:0, one launch (start us, length us, event | category | flops | bytes accessed | tf_op | source)
XLA Modules:
  0.0 6876.4 jit_solution(11239902157937228378)
XLA Ops:
  11.2 42.6 all-reduce.5
  55.1 36.3 all-gather.12.cloned.1.call-done
  97.2 73.3 %all-gather.16.cloned.1.call-done = bf16[2048,2048]{1,0:T(8,128)(2,1)} async-done(((bf16[64,2048]{1,0:T(8,128)(2,1)}), bf16[2048,2048]{1,0:T(8,128)(2,1)}) %all-gather.16.cloned.1.call-update) | async-done | bytes 8388624 | tf_op jit(solution)/shard_map/all_gather | solution.py:114
  179.2 70.3 %all-gather.20.cloned.1.call-done = bf16[2048,2048]{1,0:T(8,128)(2,1)} async-done(((bf16[64,2048]{1,0:T(8,128)(2,1)}), bf16[2048,2048]{1,0:T(8,128)(2,1)}) %all-gather.20.cloned.1.call-update) | async-done | bytes 8388624 | tf_op jit(solution)/shard_map/all_gather | solution.py:113
  255.0 69.0 %all-gather.14.cloned.1.call-done = bf16[1024,2048]{1,0:T(8,128)(2,1)} async-done(((bf16[128,2048]{1,0:T(8,128)(2,1)}), bf16[1024,2048]{1,0:T(8,128)(2,1)}) %all-gather.14.cloned.1.call-update) | async-done | bytes 4194320 | tf_op jit(solution)/shard_map/all_gather | solution.py:143
  330.4 67.8 all-gather.18.cloned.1.call-done
  423.8 53.1 all-gather.22.cloned.1.call-done
  481.9 191.5 %all-gather.24.cloned.1.call-done = bf16[2048,8192]{1,0:T(8,128)(2,1)} async-done(((bf16[64,8192]{1,0:T(8,128)(2,1)}), bf16[2048,8192]{1,0:T(8,128)(2,1)}) %all-gather.24.cloned.1.call-update) | async-done | bytes 33554448 | tf_op jit(solution)/shard_map/all_gather | solution.py:150
  691.1 178.2 %all-gather.26.cloned.1.call-done = bf16[2048,8192]{1,0:T(8,128)(2,1)} async-done(((bf16[64,8192]{1,0:T(8,128)(2,1)}), bf16[2048,8192]{1,0:T(8,128)(2,1)}) %all-gather.26.cloned.1.call-update) | async-done | bytes 33554448 | tf_op jit(solution)/shard_map/all_gather | solution.py:151
  887.2 178.2 %all-gather.28.cloned.1.call-done = bf16[8192,2048]{1,0:T(8,128)(2,1)} async-done(((bf16[256,2048]{1,0:T(8,128)(2,1)}), bf16[8192,2048]{1,0:T(8,128)(2,1)}) %all-gather.28.cloned.1.call-update) | async-done | bytes 33554448 | tf_op jit(solution)/shard_map/all_gather | solution.py:152
  1131.6 32.3 while.54
  1186.2 27.1 all-gather.32.cloned.1.call-done
  1213.3 57.8 while.55
  1291.4 25.1 fusion.81
  1316.5 25.1 fusion.82
  1342.6 25.3 fusion.45
  1403.8 46.5 all-reduce.4
  1454.0 119.8 %reduce-scatter.8.cloned.1.call-done = f32[64,2048]{1,0:T(8,128)} async-done(((f32[2048,2048]{1,0:T(8,128)}), f32[64,2048]{1,0:T(8,128)}) %reduce-scatter.8.cloned.1.call-update) | async-done | bytes 524304 | tf_op jit(solution)/shard_map/reduce_scatter | solution.py:286
  1573.7 360.3 %reduce-scatter.14.cloned.1.call-done = f32[64,2048]{1,0:T(8,128)} async-done(((f32[2048,2048]{1,0:T(8,128)}), f32[64,2048]{1,0:T(8,128)}) %reduce-scatter.14.cloned.1.call-update) | async-done | bytes 524304 | tf_op jit(solution)/shard_map/reduce_scatter | solution.py:289
  1934.0 360.1 %reduce-scatter.10.cloned.1.call-done = f32[64,2048]{1,0:T(8,128)} async-done(((f32[2048,2048]{1,0:T(8,128)}), f32[64,2048]{1,0:T(8,128)}) %reduce-scatter.10.cloned.1.call-update) | async-done | bytes 524304 | tf_op jit(solution)/shard_map/reduce_scatter | solution.py:287
  2294.1 360.1 %reduce-scatter.12.cloned.1.call-done = f32[64,2048]{1,0:T(8,128)} async-done(((f32[2048,2048]{1,0:T(8,128)}), f32[64,2048]{1,0:T(8,128)}) %reduce-scatter.12.cloned.1.call-update) | async-done | bytes 524304 | tf_op jit(solution)/shard_map/reduce_scatter | solution.py:288
  2654.1 1404.6 %reduce-scatter.16.cloned.1.call-done = f32[64,8192]{1,0:T(8,128)} async-done(((f32[2048,8192]{1,0:T(8,128)}), f32[64,8192]{1,0:T(8,128)}) %reduce-scatter.16.cloned.1.call-update) | async-done | bytes 2097168 | tf_op jit(solution)/shard_map/reduce_scatter | solution.py:182
  4058.8 1405.3 %reduce-scatter.18.cloned.1.call-done = f32[64,8192]{1,0:T(8,128)} async-done(((f32[2048,8192]{1,0:T(8,128)}), f32[64,8192]{1,0:T(8,128)}) %reduce-scatter.18.cloned.1.call-update) | async-done | bytes 2097168 | tf_op jit(solution)/shard_map/reduce_scatter | solution.py:191
  5464.1 1405.3 %reduce-scatter.20.cloned.1.call-done = f32[256,2048]{1,0:T(8,128)} async-done(((f32[8192,2048]{1,0:T(8,128)}), f32[256,2048]{1,0:T(8,128)}) %reduce-scatter.20.cloned.1.call-update) | async-done | bytes 2097168 | tf_op jit(solution)/shard_map/reduce_scatter | solution.py:176
  (227 shorter events, 354.6 us)
Async XLA Ops:
  7.2 84.2 %all-gather.12.cloned.1.call-start = ((), (), s32[]{:S(2)}) async-start(), calls=%async_computation.7 | async-start | bytes 8650752 | tf_op jit(solution)/shard_map/all_gather | solution.py:115
  7.9 162.5 %all-gather.16.cloned.1.call-start = ((), (), s32[]{:S(2)}) async-start(), calls=%async_computation.9 | async-start | bytes 8650752 | tf_op jit(solution)/shard_map/all_gather | solution.py:114
  8.7 240.8 %all-gather.20.cloned.1.call-start = ((), (), s32[]{:S(2)}) async-start(), calls=%async_computation.11 | async-start | bytes 8650752 | tf_op jit(solution)/shard_map/all_gather | solution.py:113
  9.4 314.6 %all-gather.14.cloned.1.call-start = ((), (), s32[]{:S(2)}) async-start(), calls=%async_computation.8 | async-start | bytes 4718592 | tf_op jit(solution)/shard_map/all_gather | solution.py:143
  53.8 195.7 %copy-start.21 = (f32[2048]{0:T(1024)}, f32[2048]{0:T(1024)S(1)}, u32[]{:S(2)}) copy-start(f32[2048]{0:T(1024)S(1)} %convert_element_type.160) | copy-start | bytes 24580
  55.0 194.4 %copy-start.26 = (f32[128]{0:T(128)}, f32[128]{0:T(128)S(1)}, u32[]{:S(2)}) copy-start(f32[128]{0:T(128)S(1)} %fusion.66) | copy-start | bytes 1540
  55.1 115.4 %copy-start.1 = (bf16[1,128,2048]{2,1,0:T(8,128)(2,1)S(1)}, bf16[1,128,2048]{2,1,0:T(8,128)(2,1)}, u32[]{:S(2)}) copy-start(bf16[1,128,2048]{2,1,0:T(8,128)(2,1)} %param.18) | copy-start | bytes 1572868
  97.1 301.1 %all-gather.18.cloned.1.call-start = ((), (), s32[]{:S(2)}) async-start(), calls=%async_computation.10 | async-start | bytes 4718592 | tf_op jit(solution)/shard_map/all_gather | solution.py:142
  175.9 301.0 %all-gather.22.cloned.1.call-start = ((), (), s32[]{:S(2)}) async-start(), calls=%async_computation.12 | async-start | bytes 8650752 | tf_op jit(solution)/shard_map/all_gather | solution.py:116
  176.5 496.8 %all-gather.24.cloned.1.call-start = ((), (), s32[]{:S(2)}) async-start(), calls=%async_computation.13 | async-start | bytes 34603008 | tf_op jit(solution)/shard_map/all_gather | solution.py:150
  177.3 692.1 %all-gather.26.cloned.1.call-start = ((), (), s32[]{:S(2)}) async-start(), calls=%async_computation.14 | async-start | bytes 34603008 | tf_op jit(solution)/shard_map/all_gather | solution.py:151
  178.0 887.3 %all-gather.28.cloned.1.call-start = ((), (), s32[]{:S(2)}) async-start(), calls=%async_computation.15 | async-start | bytes 34603008 | tf_op jit(solution)/shard_map/all_gather | solution.py:152
  178.7 1007.5 %all-gather.30.cloned.1.call-start = ((), (), s32[]{:S(2)}) async-start(), calls=%async_computation.16 | async-start | bytes 4718592 | tf_op jit(solution)/shard_map/all_gather | solution.py:268
  255.0 958.3 %all-gather.32.cloned.1.call-start = ((), (), s32[]{:S(2)}) async-start(), calls=%async_computation.17 | async-start | bytes 4718592 | tf_op jit(solution)/shard_map/all_gather | solution.py:269
  481.7 639.9 %copy-start.8 = (f32[128,2048]{1,0:T(8,128)}, f32[128,2048]{1,0:T(8,128)S(1)}, u32[]{:S(2)}) copy-start(f32[128,2048]{1,0:T(8,128)S(1)} %get-tuple-element.1446) | copy-start | bytes 3145732
  481.8 387.5 %copy-start.13 = (bf16[128,2048]{1,0:T(8,128)(2,1)}, bf16[128,2048]{1,0:T(8,128)(2,1)S(1)}, u32[]{:S(2)}) copy-start(bf16[128,2048]{1,0:T(8,128)(2,1)S(1)} %multiply_convert_fusion.3) | copy-start | bytes 1572868
  691.1 374.2 %copy-start.23 = (bf16[1,128,2048]{2,1,0:T(8,128)(2,1)S(1)}, bf16[1,128,2048]{2,1,0:T(8,128)(2,1)}, u32[]{:S(2)}) copy-start(bf16[1,128,2048]{2,1,0:T(8,128)(2,1)} %param.29) | copy-start | bytes 1572868
  1131.5 442.2 %reduce-scatter.8.cloned.1.call-start = ((), (), s32[]{:S(2)}) async-start(), calls=%async_computation.18 | async-start | bytes 17301504 | tf_op jit(solution)/shard_map/reduce_scatter | solution.py:286
  1173.6 760.4 %reduce-scatter.14.cloned.1.call-start = ((), (), s32[]{:S(2)}) async-start(), calls=%async_computation.21 | async-start | bytes 17301504 | tf_op jit(solution)/shard_map/reduce_scatter | solution.py:289
  1183.3 1110.7 %reduce-scatter.10.cloned.1.call-start = ((), (), s32[]{:S(2)}) async-start(), calls=%async_computation.19 | async-start | bytes 17301504 | tf_op jit(solution)/shard_map/reduce_scatter | solution.py:287
  1280.8 1373.4 %reduce-scatter.12.cloned.1.call-start = ((), (), s32[]{:S(2)}) async-start(), calls=%async_computation.20 | async-start | bytes 17301504 | tf_op jit(solution)/shard_map/reduce_scatter | solution.py:288
  1290.3 2768.4 %reduce-scatter.16.cloned.1.call-start = ((), (), s32[]{:S(2)}) async-start(), calls=%async_computation.22 | async-start | bytes 69206016 | tf_op jit(solution)/shard_map/reduce_scatter | solution.py:182
  1316.4 4147.6 %reduce-scatter.18.cloned.1.call-start = ((), (), s32[]{:S(2)}) async-start(), calls=%async_computation.23 | async-start | bytes 69206016 | tf_op jit(solution)/shard_map/reduce_scatter | solution.py:191
  1341.6 5527.8 %reduce-scatter.20.cloned.1.call-start = ((), (), s32[]{:S(2)}) async-start(), calls=%async_computation.24 | async-start | bytes 69206016 | tf_op jit(solution)/shard_map/reduce_scatter | solution.py:176
  (26 other events, 427.5 us)
Sparse Core Ops, SparseCore 0:
  11.0 80.3 all-gather.11
  94.4 75.9 all-gather.15
  173.4 75.9 all-gather.19
  252.0 71.9 all-gather.13
  326.6 71.6 all-gather.17
  401.1 75.7 all-gather.21
  479.9 193.3 all-gather.23
  676.3 192.9 all-gather.25
  872.3 192.9 all-gather.27
  1067.9 71.5 all-gather.29
  1141.6 71.6 all-gather.31
  1216.0 357.6 reduce-scatter.7
  1576.6 357.3 reduce-scatter.13
  1936.7 357.3 reduce-scatter.9
  2296.8 357.3 reduce-scatter.11
  2656.9 1401.8 reduce-scatter.15
  4061.6 1402.4 reduce-scatter.17
  5466.9 1402.5 reduce-scatter.19
where the time goes:
time: 6890 us; the launch traced here: 6880 us
  waiting for transfers between devices  6370 us (92%)
  matrix products  310 us (4%)
  blocking collectives  89.1 us (1%)
  local copies, waits for them, and re-layouts  74.5 us (1%)
    reduce_scatter x1, waiting for transfers between devices, local(): lax.psum_scatter(grad_down, ('row', 'seq'), scatter_dimension=0, tiled=True)  1410 us
    reduce_scatter x1, waiting for transfers between devices, local(): lax.psum_scatter(grad_up, ('row', 'seq'), scatter_dimension=0, tiled=True)  1410 us
    reduce_scatter x1, waiting for transfers between devices, local(): lax.psum_scatter(grad_gate, ('row', 'seq'), scatter_dimension=0, tiled=True)  1400 us
    reduce_scatter x1, waiting for transfers between devices, local(): lax.psum_scatter(grad_out, ('row', 'seq'), scatter_dimension=0, tiled=True)  360 us
    reduce_scatter x1, waiting for transfers between devices, local(): lax.psum_scatter(grad_key, ('row', 'seq'), scatter_dimension=0, tiled=True)  360 us
    reduce_scatter x1, waiting for transfers between devices, local(): lax.psum_scatter(grad_value, ('row', 'seq'), scatter_dimension=0, tiled=T...  360 us
    all_gather x1, waiting for transfers between devices, local(): lax.all_gather(w_gate, ('row', 'seq'), axis=0, tiled=True)  191 us
    all_gather x1, waiting for transfers between devices, local(): lax.all_gather(w_up, ('row', 'seq'), axis=0, tiled=True)  178 us
  transfers between devices with their start and end apart: 18, of which 17 were waited for; matrix products, arithmetic and copies ran while one was open for 6% of the time, Pallas kernels for 0%

commit v1 on v0

--- a/solution.py
+++ b/solution.py
@@ -1,6 +1,10 @@
+import functools
+
 import jax
 import jax.numpy as jnp
 from jax import lax
+from jax.experimental import pallas as pl
+from jax.experimental.pallas import tpu as pltpu
 from jax.sharding import PartitionSpec as P
 
 HEADS = 16
@@ -74,7 +78,7 @@
     return lax.fori_loop(0, block_count, turn_over, running)
 
 
-def local(
+def gathered_local(
     inputs,
     lengths,
     w_query,
@@ -304,6 +308,872 @@
     )
 
 
+MESH = pl.DeviceIdType.MESH
+VMEM_BYTES = 60 * 1024 * 1024
+
+
+class Place:
+    def __init__(self, row_count, seq_count):
+        self.row_count, self.seq_count = row_count, seq_count
+        self.r, self.s = lax.axis_index("row"), lax.axis_index("seq")
+        self.n_hi = seq_count // 2
+        self.hi, self.lo = self.s // 2, lax.rem(self.s, 2)
+        self.r_core = self.r + 1 - 2 * lax.rem(self.r, 2)
+        self.r_y = lax.rem(self.r + 2, 4)
+        self.r_far = lax.rem(self.r_core + 2, 4)
+        self.side = (self.r, self.s + 1 - 2 * self.lo)
+        self.up = (self.r, self.s + 2)
+        self.down = (self.r, self.s - 2)
+        self.core = (self.r_core, self.s)
+        self.y = (self.r_y, self.s)
+        self.has_up = self.hi < self.n_hi - 1
+        self.has_down = self.hi > 0
+
+    def peer(self, step):
+        return lax.rem(self.s + step, self.seq_count)
+
+    def chain(self):
+        return [(None, self.side), (self.has_up, self.up), (self.has_down, self.down)]
+
+    def peers(self):
+        return [(None, (self.r, self.peer(step))) for step in range(1, self.seq_count)]
+
+    def rows(self):
+        return [(None, self.core), (None, self.y)]
+
+
+def greet(devices):
+    barrier = pltpu.get_barrier_semaphore()
+    total = 0
+    for condition, device in devices:
+        if condition is None:
+            pl.semaphore_signal(barrier, inc=1, device_id=device, device_id_type=MESH)
+            total = total + 1
+        else:
+
+            @pl.when(condition)
+            def _(device=device):
+                pl.semaphore_signal(barrier, inc=1, device_id=device, device_id_type=MESH)
+
+            total = total + condition.astype(jnp.int32)
+    pl.semaphore_wait(barrier, total)
+
+
+class Sems:
+    def __init__(self, ref):
+        self.ref, self.used = ref, 0
+
+    def take(self, count):
+        base = self.used
+        self.used += count
+        assert self.used <= self.ref.shape[0], self.used
+        return lambda index: self.ref.at[base + index]
+
+
+def push(source, target, send, recv, device):
+    pltpu.make_async_remote_copy(
+        src_ref=source, dst_ref=target, send_sem=send, recv_sem=recv, device_id=device, device_id_type=MESH
+    ).start()
+
+
+def settle(ref, sem):
+    pltpu.make_async_copy(ref, ref, sem).wait()
+
+
+def no_op(block):
+    return None
+
+
+class SeqGather:
+    def __init__(self, place, sems, source, at, arrived=no_op):
+        self.p, self.source, self.at, self.arrived = place, source, at, arrived
+        n = place.n_hi
+        self.own, self.up, self.down = sems.take(1), sems.take(n), sems.take(n)
+        self.side, self.recv = sems.take(n), sems.take(2 * n)
+
+    def start(self):
+        p, s = self.p, self.p.s
+        pltpu.make_async_copy(self.source, self.at(s), self.own(0)).start()
+
+        @pl.when(p.has_up)
+        def _():
+            push(self.source, self.at(s), self.up(0), self.recv(s), p.up)
+
+        @pl.when(p.has_down)
+        def _():
+            push(self.source, self.at(s), self.down(0), self.recv(s), p.down)
+
+        push(self.source, self.at(s), self.side(p.hi), self.recv(s), p.side)
+
+    def step(self, k):
+        p = self.p
+
+        @pl.when(p.hi >= k)
+        def _():
+            block = p.s - 2 * k
+            settle(self.at(block), self.recv(block))
+
+            @pl.when(p.has_up)
+            def _():
+                push(self.at(block), self.at(block), self.up(k), self.recv(block), p.up)
+
+            push(self.at(block), self.at(block), self.side(p.hi - k), self.recv(block), p.side)
+            self.arrived(block)
+
+        @pl.when(p.hi + k < p.n_hi)
+        def _():
+            block = p.s + 2 * k
+            settle(self.at(block), self.recv(block))
+
+            @pl.when(p.has_down)
+            def _():
+                push(self.at(block), self.at(block), self.down(k), self.recv(block), p.down)
+
+            push(self.at(block), self.at(block), self.side(p.hi + k), self.recv(block), p.side)
+            self.arrived(block)
+
+    def aside(self, k):
+        p = self.p
+        if k == 0:
+            block = 2 * p.hi + 1 - p.lo
+            settle(self.at(block), self.recv(block))
+            self.arrived(block)
+            return
+
+        @pl.when(p.hi >= k)
+        def _():
+            block = 2 * (p.hi - k) + 1 - p.lo
+            settle(self.at(block), self.recv(block))
+            self.arrived(block)
+
+        @pl.when(p.hi + k < p.n_hi)
+        def _():
+            block = 2 * (p.hi + k) + 1 - p.lo
+            settle(self.at(block), self.recv(block))
+            self.arrived(block)
+
+    def finish(self):
+        p = self.p
+        settle(self.source, self.own(0))
+        for k in range(p.n_hi):
+
+            @pl.when(p.has_up & (p.hi >= k))
+            def _():
+                settle(self.source, self.up(k))
+
+            @pl.when(p.has_down & (p.hi + k < p.n_hi))
+            def _():
+                settle(self.source, self.down(k))
+
+            settle(self.source, self.side(k))
+
+
+class SeqExchange:
+    def __init__(self, place, sems, piece, at, arrived=no_op):
+        self.p, self.piece, self.at, self.arrived = place, piece, at, arrived
+        n = place.seq_count
+        self.own, self.send, self.recv = sems.take(1), sems.take(n), sems.take(n)
+
+    def start_own(self):
+        s = self.p.s
+        pltpu.make_async_copy(self.piece(s), self.at(s), self.own(0)).start()
+
+    def start(self):
+        p, s = self.p, self.p.s
+        self.start_own()
+        for step in range(1, p.seq_count):
+            t = p.peer(step)
+            push(self.piece(t), self.at(s), self.send(step), self.recv(s), (p.r, t))
+
+    def step(self, step):
+        block = self.p.peer(self.p.seq_count - step)
+        settle(self.at(block), self.recv(block))
+        self.arrived(block)
+
+    def finish(self):
+        p = self.p
+        settle(self.at(p.s), self.own(0))
+        for step in range(1, p.seq_count):
+            settle(self.at(p.s), self.send(step))
+
+
+class RowForward:
+    def __init__(self, place, sems, blocks, at):
+        self.p, self.at, self.blocks = place, at, blocks
+        self.core, self.y, self.far = sems.take(blocks), sems.take(blocks), sems.take(blocks)
+        self.from_core, self.from_y, self.from_far = sems.take(blocks), sems.take(blocks), sems.take(blocks)
+
+    def forward(self, block, source=None):
+        p = self.p
+        source = self.at(p.r, block) if source is None else source
+        push(source, self.at(p.r, block), self.y(block), self.from_y(block), p.y)
+        push(source, self.at(p.r, block), self.core(block), self.from_core(block), p.core)
+
+    def relay(self, block):
+        p = self.p
+        settle(self.at(p.r_y, block), self.from_y(block))
+        push(self.at(p.r_y, block), self.at(p.r_y, block), self.far(block), self.from_far(block), p.core)
+
+    def finish(self):
+        p = self.p
+        for block in range(self.blocks):
+            settle(self.at(p.r_core, block), self.from_core(block))
+            settle(self.at(p.r_far, block), self.from_far(block))
+            settle(self.at(p.r, block), self.core(block))
+            settle(self.at(p.r, block), self.y(block))
+            settle(self.at(p.r_y, block), self.far(block))
+
+
+def add_into(target, *sources):
+    @pl.loop(0, target.shape[0] // 16)
+    def _(tile):
+        rows = pl.ds(pl.multiple_of(tile * 16, 16), 16)
+        total = sources[0][rows, :].astype(jnp.float32)
+        for source in sources[1:]:
+            total = total + source[rows, :].astype(jnp.float32)
+        target[rows, :] = total.astype(target.dtype)
+
+
+def add_small(target, *sources):
+    total = sources[0][...].astype(jnp.float32)
+    for source in sources[1:]:
+        total = total + source[...].astype(jnp.float32)
+    target[...] = total.astype(target.dtype)
+
+
+class SeqReduce:
+    def __init__(self, place, sems, at, side_slot, chain_slot, target, add=add_into):
+        self.p, self.at, self.add, self.target = place, at, add, target
+        self.side_slot, self.chain_slot = side_slot, chain_slot
+        n = place.n_hi
+        self.side, self.from_side = sems.take(n), sems.take(n)
+        self.send, self.recv = sems.take(n), sems.take(2 * n)
+
+    def turn(self, t):
+        p = self.p
+        n, hi = p.n_hi, p.hi
+        low = jnp.where(t < n - 1 - hi, n - 1 - t, t - (n - 1 - hi))
+        high = jnp.where(t < hi, t, n - 1 - (t - hi))
+        return jnp.where(hi < n // 2, low, high)
+
+    def start(self, t):
+        p, block = self.p, self.turn(t)
+        push(self.at(2 * block + 1 - p.lo), self.side_slot(block), self.side(block), self.from_side(block), p.side)
+
+    def step(self, t):
+        p, n, block = self.p, self.p.n_hi, self.turn(t)
+        mine, got = self.at(2 * block + p.lo), self.side_slot(block)
+        settle(got, self.from_side(block))
+        if t == n - 1:
+            return self.close()
+
+        @pl.when(block > p.hi)
+        def _():
+            @pl.when(p.has_down)
+            def _():
+                settle(got, self.recv(block))
+                self.add(got, mine, got, self.chain_slot(0, block))
+
+            @pl.when(jnp.logical_not(p.has_down))
+            def _():
+                self.add(got, mine, got)
+
+            push(got, self.chain_slot(0, block), self.send(block), self.recv(block), p.up)
+
+        @pl.when(block < p.hi)
+        def _():
+            @pl.when(p.has_up)
+            def _():
+                settle(got, self.recv(n + block))
+                self.add(got, mine, got, self.chain_slot(1, block))
+
+            @pl.when(jnp.logical_not(p.has_up))
+            def _():
+                self.add(got, mine, got)
+
+            push(got, self.chain_slot(1, block), self.send(block), self.recv(n + block), p.down)
+
+    def close(self):
+        p, n, hi = self.p, self.p.n_hi, self.p.hi
+        mine, got = self.at(p.s), self.side_slot(hi)
+        below, above = self.chain_slot(0, hi), self.chain_slot(1, hi)
+
+        @pl.when(p.has_down)
+        def _():
+            settle(got, self.recv(hi))
+
+        @pl.when(p.has_up)
+        def _():
+            settle(got, self.recv(n + hi))
+
+        @pl.when(p.has_down & p.has_up)
+        def _():
+            self.add(self.target, mine, got, below, above)
+
+        @pl.when(p.has_down & jnp.logical_not(p.has_up))
+        def _():
+            self.add(self.target, mine, got, below)
+
+        @pl.when(jnp.logical_not(p.has_down))
+        def _():
+            self.add(self.target, mine, got, above)
+
+    def finish(self):
+        p = self.p
+        for block in range(p.n_hi):
+            settle(self.side_slot(block), self.side(block))
+
+            @pl.when(p.hi != block)
+            def _():
+                settle(self.side_slot(block), self.send(block))
+
+
+class RowReduce:
+    def __init__(self, place, sems, blocks, at, core_slot, y_slot, target, add=add_into):
+        self.p, self.at, self.add, self.target = place, at, add, target
+        self.core_slot, self.y_slot, self.blocks = core_slot, y_slot, blocks
+        self.send, self.recv = sems.take(2 * blocks), sems.take(2 * blocks)
+        self.y, self.from_y = sems.take(blocks), sems.take(blocks)
+
+    def start(self, block):
+        p, n = self.p, self.blocks
+        push(self.at(p.r_far, block), self.core_slot(0, block), self.send(block), self.recv(block), p.core)
+        push(self.at(p.r_core, block), self.core_slot(1, block), self.send(n + block), self.recv(n + block), p.core)
+
+    def step(self, block):
+        p = self.p
+        got = self.core_slot(0, block)
+        settle(got, self.recv(block))
+        self.add(got, self.at(p.r_y, block), got)
+        push(got, self.y_slot(block), self.y(block), self.from_y(block), p.y)
+
+    def close(self, block):
+        p = self.p
+        settle(self.core_slot(1, block), self.recv(self.blocks + block))
+        settle(self.y_slot(block), self.from_y(block))
+        self.add(self.target(block), self.at(p.r, block), self.core_slot(1, block), self.y_slot(block))
+
+    def finish(self):
+        n = self.blocks
+        for block in range(n):
+            settle(self.core_slot(0, block), self.send(block))
+            settle(self.core_slot(1, block), self.send(n + block))
+            settle(self.core_slot(0, block), self.y(block))
+
+
+def columns(ref, index, width):
+    return ref.at[:, pl.ds(pl.multiple_of(index * width, width), width)]
+
+
+def call(kernel, shapes, ident, args, spaces, out_spaces, scratch, sems):
+    return pl.pallas_call(
+        kernel,
+        out_shape=shapes,
+        in_specs=[pl.BlockSpec(memory_space=space) for space in spaces],
+        out_specs=jax.tree.map(lambda space: pl.BlockSpec(memory_space=space), out_spaces),
+        scratch_shapes=list(scratch) + [pltpu.SemaphoreType.DMA((sems,))],
+        compiler_params=pltpu.CompilerParams(
+            collective_id=ident, has_side_effects=True, vmem_limit_bytes=VMEM_BYTES
+        ),
+    )(*args)
+
+
+def shape_of(dims, dtype=jnp.bfloat16):
+    return jax.ShapeDtypeStruct(dims, dtype)
+
+
+def opening_kernel(rows, seqs, x, g, wqkv, wgu, wdown, wout, gains, xs, gs, vqkv, vgu, vdown, vout, vgains, sems):
+    p, pool = Place(rows, seqs), Sems(sems)
+    greet(p.peers() + p.rows())
+    half = x.shape[0] // 2
+    down_blocks, down_rows = vdown.shape[1], vdown.shape[2]
+
+    def part(source, target, c):
+        piece = pl.ds(c * half, half)
+        return SeqGather(p, pool, source.at[piece], lambda b: target.at[b, piece])
+
+    qkv_rows = RowForward(p, pool, seqs, lambda r, b: vqkv.at[r, b])
+    gu_rows = RowForward(p, pool, seqs, lambda r, b: vgu.at[r, b])
+    down_fwd = RowForward(p, pool, down_blocks, lambda r, b: vdown.at[r, b])
+    out_rows = RowForward(p, pool, seqs, lambda r, b: vout.at[r, b])
+    gain_rows = RowForward(p, pool, seqs, lambda r, b: vgains.at[r, b])
+    x_parts = [part(x, xs, c) for c in range(2)]
+    g_parts = [part(g, gs, c) for c in range(2)]
+    qkv = SeqExchange(p, pool, lambda t: wqkv.at[t], lambda b: vqkv.at[p.r, b], qkv_rows.forward)
+    gu = SeqExchange(p, pool, lambda t: wgu.at[t], lambda b: vgu.at[p.r, b], gu_rows.forward)
+    out = SeqGather(p, pool, wout, lambda b: vout.at[p.r, b], out_rows.forward)
+    gain = SeqGather(p, pool, gains, lambda b: vgains.at[p.r, b], gain_rows.forward)
+    down_own = pool.take(1)
+
+    gain.start()
+    gain_rows.forward(p.s, gains)
+    qkv.start()
+    qkv_rows.forward(p.s, wqkv.at[p.s])
+    for member in x_parts:
+        member.start()
+    pltpu.make_async_copy(wdown, vdown.at[p.r], down_own(0)).start()
+    for block in range(down_blocks):
+        down_fwd.forward(block, wdown.at[block])
+    gu_rows.forward(p.s, wgu.at[p.s])
+    out_rows.forward(p.s, wout)
+    gu.start()
+    out.start()
+    for member in g_parts:
+        member.start()
+    gathers = [gain] + x_parts + [out] + g_parts
+    for k in range(1, p.n_hi):
+        for member in gathers:
+            member.step(k)
+        for step in (2 * k - 1, 2 * k):
+            qkv.step(step)
+            gu.step(step)
+    qkv.step(seqs - 1)
+    gu.step(seqs - 1)
+    for k in range(p.n_hi):
+        for member in gathers:
+            member.aside(k)
+    for member in (gain_rows, qkv_rows, down_fwd, gu_rows, out_rows):
+        for block in range(member.blocks):
+            member.relay(block)
+    for member in gathers + [qkv, gu, gain_rows, qkv_rows, down_fwd, gu_rows, out_rows]:
+        member.finish()
+    settle(wdown, down_own(0))
+
+
+def opening(rows, seqs, x, g, wqkv, wgu, wdown, wout, gains):
+    tokens, width = x.shape
+    wdown = wdown.reshape(4, wdown.shape[0] // 4, width)
+    args = (x, g, wqkv, wgu, wdown, wout, gains)
+    shapes = (
+        shape_of((seqs, tokens, width)),
+        shape_of((seqs, tokens, width)),
+        shape_of((rows,) + wqkv.shape),
+        shape_of((rows,) + wgu.shape),
+        shape_of((rows,) + wdown.shape),
+        shape_of((rows, seqs) + wout.shape),
+        shape_of((rows, seqs) + gains.shape, jnp.float32),
+    )
+    return call(
+        functools.partial(opening_kernel, rows, seqs), shapes, 1, args, [pl.ANY] * 7, (pl.ANY,) * 7, [], 640
+    )
+
+
+def spread_kernel(rows, seqs, source, target, sems):
+    p, pool = Place(rows, seqs), Sems(sems)
+    greet(p.chain())
+    half = source.shape[0] // 2
+    members = []
+    for c in range(2):
+        piece = pl.ds(c * half, half)
+        members.append(SeqGather(p, pool, source.at[piece], lambda b, piece=piece: target.at[b, piece]))
+    for member in members:
+        member.start()
+    for k in range(1, p.n_hi):
+        for member in members:
+            member.step(k)
+    for k in range(p.n_hi):
+        for member in members:
+            member.aside(k)
+    for member in members:
+        member.finish()
+
+
+def spread(rows, seqs, ident, source):
+    return call(
+        functools.partial(spread_kernel, rows, seqs),
+        shape_of((seqs,) + source.shape),
+        ident,
+        (source,),
+        [pltpu.VMEM],
+        pltpu.VMEM,
+        [],
+        128,
+    )
+
+
+def to_tokens_kernel(rows, seqs, source, target, sems):
+    p, pool = Place(rows, seqs), Sems(sems)
+    greet(p.peers())
+    width = source.shape[2]
+    member = SeqExchange(p, pool, lambda t: source.at[t], lambda b: columns(target, b, width))
+    member.start()
+    for step in range(1, seqs):
+        member.step(step)
+    member.finish()
+
+
+def to_heads_kernel(rows, seqs, source, target, sems):
+    p, pool = Place(rows, seqs), Sems(sems)
+    greet(p.peers())
+    width = target.shape[2]
+    member = SeqExchange(p, pool, lambda t: columns(source, t, width), lambda b: target.at[b])
+    member.start()
+    for step in range(1, seqs):
+        member.step(step)
+    member.finish()
+
+
+def to_tokens(rows, seqs, ident, source):
+    tokens = source.shape[0] // seqs
+    width = source.shape[1]
+    return call(
+        functools.partial(to_tokens_kernel, rows, seqs),
+        shape_of((tokens, width * seqs)),
+        ident,
+        (source.reshape(seqs, tokens, width),),
+        [pltpu.VMEM],
+        pltpu.VMEM,
+        [],
+        64,
+    )
+
+
+def to_heads(rows, seqs, ident, source):
+    tokens, width = source.shape[0], source.shape[1] // seqs
+    return call(
+        functools.partial(to_heads_kernel, rows, seqs),
+        shape_of((seqs, tokens, width)),
+        ident,
+        (source,),
+        [pltpu.VMEM],
+        pltpu.VMEM,
+        [],
+        64,
+    ).reshape(seqs * tokens, width)
+
+
+def reduce_kernel(rows, seqs, count, *refs):
+    p = Place(rows, seqs)
+    sources, targets = refs[:count], refs[count : 2 * count]
+    side, chain, sems = refs[2 * count :]
+    pool = Sems(sems)
+    greet(p.chain())
+    half = targets[0].shape[0] // 2
+    members = []
+    for number in range(count):
+        for c in range(2):
+            piece = pl.ds(c * half, half)
+            members.append(
+                SeqReduce(
+                    p,
+                    pool,
+                    lambda b, n=number, piece=piece: sources[n].at[b, piece],
+                    lambda b, n=number, piece=piece: side.at[n, b, piece],
+                    lambda w, b, n=number, piece=piece: chain.at[n, w, b, piece],
+                    targets[number].at[piece],
+                )
+            )
+    for first in range(0, len(members), 2):
+        for t in range(p.n_hi):
+            for member in members[first : first + 2]:
+                member.start(t)
+    for first in range(0, len(members), 2):
+        for t in range(p.n_hi):
+            for member in members[first : first + 2]:
+                member.step(t)
+    for member in members:
+        member.finish()
+
+
+def reduced(rows, seqs, ident, sources):
+    count = len(sources)
+    tokens, width = sources[0].shape[0] // seqs, sources[0].shape[1]
+    sources = [source.reshape(seqs, tokens, width) for source in sources]
+    return call(
+        functools.partial(reduce_kernel, rows, seqs, count),
+        (shape_of((tokens, width), jnp.float32),) * count,
+        ident,
+        sources,
+        [pltpu.VMEM] * count,
+        (pltpu.VMEM,) * count,
+        [
+            pltpu.VMEM((count, seqs // 2, tokens, width), jnp.bfloat16),
+            pltpu.VMEM((count, 2, seqs // 2, tokens, width), jnp.bfloat16),
+        ],
+        256,
+    )
+
+
+def closing_kernel(
+    rows,
+    seqs,
+    qkv,
+    gu,
+    down,
+    out,
+    gain,
+    qkv_got,
+    gu_got,
+    down_sum,
+    out_sum,
+    gain_sum,
+    qkv_core,
+    gu_core,
+    down_core,
+    out_core,
+    gain_core,
+    qkv_y,
+    gu_y,
+    down_y,
+    out_y,
+    gain_y,
+    out_side,
+    out_chain,
+    gain_side,
+    gain_chain,
+    sems,
+):
+    p, pool = Place(rows, seqs), Sems(sems)
+    greet(p.peers() + p.rows())
+
+    def over_rows(source, core_slots, y_slots, target, add=add_into):
+        return RowReduce(
+            p,
+            pool,
+            source.shape[1],
+            lambda r, b: source.at[r, b],
+            lambda w, b: core_slots.at[w, b],
+            lambda b: y_slots.at[b],
+            target,
+            add,
+        )
+
+    qkv_rows = over_rows(qkv, qkv_core, qkv_y, lambda b: qkv_y.at[b])
+    gu_rows = over_rows(gu, gu_core, gu_y, lambda b: gu_y.at[b])
+    down_rows = over_rows(down, down_core, down_y, lambda b: down_sum.at[b])
+    out_rows = over_rows(out, out_core, out_y, lambda b: out_y.at[b])
+    gain_rows = over_rows(gain, gain_core, gain_y, lambda b: gain_y.at[b], add_small)
+    qkv_swap = SeqExchange(p, pool, lambda t: qkv_y.at[t], lambda b: qkv_got.at[b])
+    gu_swap = SeqExchange(p, pool, lambda t: gu_y.at[t], lambda b: gu_got.at[b])
+    out_seq = SeqReduce(
+        p,
+        pool,
+        lambda b: out_y.at[b],
+        lambda b: out_side.at[b],
+        lambda w, b: out_chain.at[w, b],
+        out_sum,
+    )
+    gain_seq = SeqReduce(
+        p,
+        pool,
+        lambda b: gain_y.at[b],
+        lambda b: gain_side.at[b],
+        lambda w, b: gain_chain.at[w, b],
+        gain_sum,
+        add_small,
+    )
+    members = (gain_rows, gu_rows, qkv_rows, out_rows, down_rows)
+    for member in members:
+        for block in range(member.blocks):
+            member.start(block)
+    for member in members:
+        for block in range(member.blocks):
+            member.step(block)
+    for block in range(seqs):
+        gain_rows.close(block)
+    for t in range(p.n_hi):
+        gain_seq.start(t)
+    for block in range(seqs):
+        gu_rows.close(block)
+    gu_swap.start()
+    for block in range(seqs):
+        qkv_rows.close(block)
+    qkv_swap.start()
+    for block in range(seqs):
+        out_rows.close(block)
+    for t in range(p.n_hi):
+        out_seq.start(t)
+    for block in range(down_rows.blocks):
+        down_rows.close(block)
+    for t in range(p.n_hi):
+        gain_seq.step(t)
+        out_seq.step(t)
+    for step in range(1, seqs):
+        gu_swap.step(step)
+        qkv_swap.step(step)
+    for member in members + (gu_swap, qkv_swap, out_seq, gain_seq):
+        member.finish()
+
+
+def closing(rows, seqs, qkv, gu, down, out, gain):
+    def blocks_of(array, count):
+        return array.reshape(rows, count, array.shape[0] // (rows * count), array.shape[1])
+
+    qkv, gu, out, gain = (blocks_of(array, seqs) for array in (qkv, gu, out, gain))
+    down = blocks_of(down, 4)
+    args = (qkv, gu, down, out, gain)
+
+    def slots(array, copies):
+        return pltpu.VMEM(copies + array.shape[1:], array.dtype)
+
+    half = seqs // 2
+    shapes = (
+        shape_of(qkv.shape[1:]),
+        shape_of(gu.shape[1:]),
+        shape_of(down.shape[1:], jnp.float32),
+        shape_of(out.shape[2:], jnp.float32),
+        shape_of(gain.shape[2:], jnp.float32),
+    )
+    scratch = [slots(array, (2,)) for array in args] + [slots(array, ()) for array in args]
+    for array in (out, gain):
+        scratch.append(pltpu.VMEM((half,) + array.shape[2:], array.dtype))
+        scratch.append(pltpu.VMEM((2, half) + array.shape[2:], array.dtype))
+    return call(
+        functools.partial(closing_kernel, rows, seqs),
+        shapes,
+        9,
+        args,
+        [pltpu.VMEM] * 5,
+        (pl.ANY, pl.ANY, pltpu.VMEM, pltpu.VMEM, pltpu.VMEM),
+        scratch,
+        480,
+    )
+
+
+def dot(left, right, left_axis=1, right_axis=0):
+    return lax.dot_general(
+        left, right, (((left_axis,), (right_axis,)), ((), ())), preferred_element_type=jnp.float32
+    )
+
+
+def split_local(
+    rows,
+    seqs,
+    inputs,
+    lengths,
+    w_query,
+    w_key,
+    w_value,
+    w_out,
+    gain_attn,
+    w_gate,
+    w_up,
+    w_down,
+    gain_mlp,
+    cotangent,
+):
+    low, f32 = jnp.bfloat16, jnp.float32
+    tokens, width = inputs.shape[1], inputs.shape[2]
+    deep = w_query.shape[0]
+    row_tokens = tokens * seqs
+    head_size = width // HEADS
+    scale = head_size ** (-0.5)
+    own_width = width // seqs
+    hidden_own = w_gate.shape[1] // seqs
+    heads_own = HEADS // seqs
+    hidden_block = hidden_own // rows
+
+    def by_heads(weight):
+        return weight.reshape(deep, seqs, own_width).transpose(1, 0, 2)
+
+    def by_hidden(weight):
+        return (
+            weight.reshape(deep, rows, seqs, hidden_block).transpose(2, 0, 1, 3).reshape(seqs, deep, hidden_own)
+        )
+
+    wqkv = jnp.concatenate([by_heads(w_query), by_heads(w_key), by_heads(w_value)], axis=2)
+    wgu = jnp.concatenate([by_hidden(w_gate), by_hidden(w_up)], axis=2)
+    gains_own = jnp.concatenate([gain_attn, gain_mlp]).astype(f32)[None, :]
+    gains_own = jnp.broadcast_to(gains_own, (8, 2 * deep))
+    x_low, g_low = inputs[0], cotangent[0]
+    x_all, g_all, wqkv, wgu, wdown, wout, gains = opening(
+        rows, seqs, x_low, g_low, wqkv, wgu, w_down, w_out, gains_own
+    )
+    gains = gains[:, :, 0, :].reshape(rows * seqs, 2, deep)
+    gain_one, gain_two = gains[:, 0].reshape(width), gains[:, 1].reshape(width)
+    wqkv = wqkv.reshape(width, 3 * own_width)
+    wgu = wgu.reshape(width, 2 * hidden_own)
+    wdown = wdown.reshape(hidden_own, width)
+    wout = wout.reshape(width, width)
+    g_all = g_all.reshape(row_tokens, width)
+
+    x_full = x_all.reshape(row_tokens, width).astype(f32)
+    hn = rms_norm(x_full, gain_one).astype(low)
+    qkv = dot(hn, wqkv).astype(low)
+    queries, keys, values = (
+        qkv[:, n * own_width : (n + 1) * own_width].reshape(row_tokens, heads_own, head_size) for n in range(3)
+    )
+    meta = layout(lengths[0], jnp.arange(row_tokens, dtype=jnp.int32), tokens, seqs)
+    segment, position, length_of = meta
+    allowed = (segment[:, None] == segment[None, :]) & (position[None, :] <= position[:, None])
+    shift = jnp.log(length_of.astype(f32))[None, :, None]
+
+    def sigmoids():
+        scores = jnp.einsum("qhd,khd->hqk", queries, keys, preferred_element_type=f32) * scale
+        return jnp.where(allowed[None], jax.nn.sigmoid(scores - shift), 0.0)
+
+    sig_low = sigmoids().astype(low)
+    attended = jnp.einsum("hqk,khd->qhd", sig_low, values, preferred_element_type=f32)
+    attended = to_tokens(rows, seqs, 2, attended.reshape(row_tokens, own_width).astype(low))
+
+    residual = x_low.astype(f32)
+    middle = residual + dot(attended, wout)
+    h2 = spread(rows, seqs, 3, rms_norm(middle, gain_two).astype(low)).reshape(row_tokens, width)
+    gate_up = dot(h2, wgu)
+    gate, up = gate_up[:, :hidden_own], gate_up[:, hidden_own:]
+    gated, gated_back = jax.vjp(lambda a, b: jax.nn.silu(a) * b, gate, up)
+    hidden = gated.astype(low)
+    out_part = dot(hidden, wdown).astype(low)
+    gate_grad, up_grad = gated_back(dot(g_all, wdown, 1, 1))
+    gu_grad = jnp.concatenate([gate_grad.astype(low), up_grad.astype(low)], axis=1)
+    h2_part = dot(gu_grad, wgu, 1, 1).astype(low)
+    grad_down = dot(hidden, g_all, 0, 0).astype(low)
+    grad_gu = dot(h2, gu_grad, 0, 0).astype(low)
+    h2_grad, out_sum = reduced(rows, seqs, 4, [h2_part, out_part])
+    output = (middle + out_sum).astype(low)
+
+    unused_two, second_back = jax.vjp(rms_norm, middle, gain_two)
+    middle_part, gain_two_grad = second_back(h2_grad)
+    middle_grad = g_low.astype(f32) + middle_part
+    branch = middle_grad.astype(low)
+    grad_out = dot(attended, branch, 0, 0).astype(low)
+    o_grad = to_heads(rows, seqs, 5, dot(branch, wout, 1, 1).astype(low))
+    o_grad = o_grad.reshape(row_tokens, heads_own, head_size)
+
+    sig = sigmoids()
+    slopes = jnp.einsum("qhd,khd->hqk", o_grad, values, preferred_element_type=f32)
+    score_grad = (slopes * sig * (1.0 - sig)).astype(low)
+    q_grad = jnp.einsum("hqk,khd->qhd", score_grad, keys, preferred_element_type=f32) * scale
+    k_grad = jnp.einsum("hqk,qhd->khd", score_grad, queries, preferred_element_type=f32) * scale
+    v_grad = jnp.einsum("hqk,qhd->khd", sig.astype(low), o_grad, preferred_element_type=f32)
+    qkv_grad = jnp.concatenate(
+        [member.reshape(row_tokens, own_width).astype(low) for member in (q_grad, k_grad, v_grad)], axis=1
+    )
+    grad_qkv = dot(hn, qkv_grad, 0, 0).astype(low)
+    (hn_grad,) = reduced(rows, seqs, 6, [dot(qkv_grad, wqkv, 1, 1).astype(low)])
+    unused_one, first_back = jax.vjp(rms_norm, residual, gain_one)
+    residual_part, gain_one_grad = first_back(hn_grad)
+    input_grad = middle_grad + residual_part
+
+    gain_grads = jnp.concatenate(
+        [gain_one_grad.reshape(rows * seqs, deep), gain_two_grad.reshape(rows * seqs, deep)], axis=1
+    )
+    gain_grads = jnp.broadcast_to(gain_grads[:, None, :], (rows * seqs, 8, 2 * deep)).reshape(-1, 2 * deep)
+    got_qkv, got_gu, sum_down, sum_out, sum_gain = closing(
+        rows, seqs, grad_qkv, grad_gu, grad_down, grad_out, gain_grads
+    )
+    got_qkv = got_qkv.reshape(seqs, deep, 3, own_width).transpose(2, 1, 0, 3).reshape(3, deep, width).astype(f32)
+    got_gu = (
+        got_gu.reshape(seqs, deep, 2, rows, hidden_block)
+        .transpose(2, 1, 3, 0, 4)
+        .reshape(2, deep, w_gate.shape[1])
+        .astype(f32)
+    )
+    return (
+        output[None],
+        input_grad[None],
+        got_qkv[0],
+        got_qkv[1],
+        got_qkv[2],
+        sum_out,
+        sum_gain[0, :deep],
+        got_gu[0],
+        got_gu[1],
+        sum_down.reshape(w_down.shape),
+        sum_gain[0, deep:],
+    )
+
+
 def solution(mesh):
     placed = (
         P("row", "seq", None),
@@ -319,6 +1189,11 @@
         P(("row", "seq")),
         P("row", "seq", None),
     )
+    row_count, seq_count = mesh.shape["row"], mesh.shape["seq"]
+    if row_count == 4 and seq_count % 2 == 0 and HEADS % seq_count == 0:
+        local = functools.partial(split_local, row_count, seq_count)
+    else:
+        local = gathered_local
     return jax.shard_map(
         local,
         mesh=mesh,

time: 6890 us -> 799 us (0.12)
  waiting for transfers between devices: 6370 us -> 0 us
  Pallas kernels: 0 us -> 606 us
  matrix products: 310 us -> 112 us
  blocking collectives: 89.1 us -> 0 us
    reduce_scatter x7 -> x0, waiting for transfers between devices: 5420 us -> none  [the longest x1 1410 us: local(): lax.psum_scatter(grad_down, ('row', 'seq'), scatter_dimension=0, tiled=True)]
    all_gather x11 -> x0, waiting for transfers between devices: 945 us -> none  [the longest x1 191 us: local(): lax.all_gather(w_gate, ('row', 'seq'), axis=0, tiled=True)]
    pallas_call x0 -> x7, Pallas kernels: none -> 606 us  [call(): pl.pallas_call(kernel, out_shape=shapes, in_specs=[pl.BlockSpec(memory_sp...]
    dot_general x33 -> x18, matrix products: 310 us -> 112 us  [the longest x12 96.6 us: dot(): lax.dot_general(left, right, (((left_axis,), (right_axis,)), ((), ())), p...]
    unnamed x2 -> x0, blocking collectives: 89.1 us -> none
  transfers between devices with their start and end apart: 18 -> 0, of which waited for: 17 -> 0; matrix products, arithmetic and copies ran while one was open for 6% -> 0% of each run, Pallas kernels for 0% -> 0%
where the time goes in v1:
time: 799 us; the launch traced here: 791 us
  Pallas kernels  606 us (76%)
  matrix products  112 us (14%)
  local copies, waits for them, and re-layouts  43.5 us (5%)
  other arithmetic  28.1 us (4%)
    pallas_call x7, Pallas kernels, call(): pl.pallas_call(kernel, out_shape=shapes, in_specs=[pl.BlockSpec(memory_sp...  606 us
    dot_general x12, matrix products, dot(): lax.dot_general(left, right, (((left_axis,), (right_axis,)), ((), ())), p...  96.6 us

profile of v1, /device:TPU:0, one launch (start us, length us, event | category | flops | bytes accessed | tf_op | source)
XLA Modules:
  0.0 791.0 jit_solution(6222541781122017163)
XLA Ops:
  15.7 197.5 %shard_map.203 = (bf16[8,128,2048]{2,1,0:T(8,128)(2,1)}, bf16[8,128,2048]{2,1,0:T(8,128)(2,1)}, bf16[4,8,64,768]{3,2,1,0:T(8,128)(2,1)}, bf16[4,8,64,2048]{3,2,1...) custom-call(bf16[128,2048]{1,0:T(8,128)(2,1)} %bitcast.153, ...), custom_call_target="tpu_custom_call" | custom-call | tf_op jit(solution)/shard_map/pallas_call | solution.py:669
  217.5 5.4 fusion.1
  224.8 3.6 convolution_convert_fusion.8
  237.2 16.8 %shard_map.204 = bf16[128,2048]{1,0:T(8,128)(2,1)} custom-call(bf16[8,128,256]{2,1,0:T(8,128)(2,1)} %copy.93.source), custom_call_target="tpu_custom_call" | custom-call | tf_op jit(solution)/shard_map/pallas_call | solution.py:669
  254.0 5.0 multiply_reduce_fusion.3
  259.9 54.1 %shard_map.205 = bf16[8,128,2048]{2,1,0:T(8,128)(2,1)} custom-call(bf16[128,2048]{1,0:T(8,128)(2,1)} %multiply_convert_fusion.4.source), custom_call_target="tpu_custom_call" | custom-call | tf_op jit(solution)/shard_map/pallas_call | solution.py:669
  314.0 14.7 %fusion.51 = f32[1024,2048]{0,1:T(8,128)} fusion(bf16[1024,2048]{1,0:T(8,128)(2,1)} %bitcast.159, bf16[2048,2048]{1,0:T(8,128)(2,1)} %bitcast.200), kind=kOutput, calls=%fused_computation.122 | convolution fusion | flops 8589934592 | bytes 20971520 | tf_op jit(solution)/shard_map/dot_general | solution.py:1034
  328.7 9.8 %fusion.4 = (bf16[1024,1024]{0,1:T(8,128)(2,1)}, bf16[1024,1024]{0,1:T(8,128)(2,1)}, bf16[1024,1024]{0,1:T(8,128)(2,1)S(1)}) fusion(f32[1024,2048]{0,1:T(8,128)} %fusion.51, bf16[1024,2048]{1,0:T(8,128)(2,1)S(1)} %bitcast.204, bf16[1024,2048]{1,0:T(8,128)(2,1)S(1)} %bitcast.202), kind=kOutput, calls=%fused_computation.12 | convolution fusion | flops 4311744512 | bytes 23068672 | tf_op jit(solution)/shard_map/dot_general | solution.py:1034
  338.5 15.1 %convolution_convert_fusion.2 = bf16[1024,2048]{1,0:T(8,128)(2,1)} fusion(bf16[2048,2048]{1,0:T(8,128)(2,1)} %bitcast.201, bf16[1024,1024]{0,1:T(8,128)(2,1)} %get-tuple-element.52, bf16[1024,1024]{0,1:T(8,128)(2,1)} %get-tuple-element.51), kind=kOutput, calls=%fused_computation.19 | convolution fusion | flops 8600420352 | bytes 16777216 | tf_op jit(solution)/shard_map/dot_general | solution.py:1034
  353.6 13.5 %convolution_convert_fusion = bf16[2048,2048]{1,0:T(8,128)(2,1)} fusion(bf16[1024,2048]{1,0:T(8,128)(2,1)S(1)} %bitcast.160, bf16[1024,1024]{0,1:T(8,128)(2,1)} %get-tuple-element.52, bf16[1024,1024]{0,1:T(8,128)(2,1)} %get-tuple-element.51), kind=kOutput, calls=%fused_computation.7 | convolution fusion | flops 8602517504 | bytes 16777216 | tf_op jit(solution)/shard_map/dot_general | solution.py:1034
  367.1 6.1 convolution_convert_fusion.4
  373.2 6.3 convolution_convert_fusion.5
  379.5 98.4 %shard_map.206 = (f32[128,2048]{1,0:T(8,128)}, f32[128,2048]{1,0:T(8,128)}) custom-call(bf16[8,128,2048]{2,1,0:T(8,128)(2,1)} %bitcast.161, bf16[8,128,2048]{2,1,0:T(8,128)(2,1)} %bitcast.162), custom_call_target="tpu_custom_call" | custom-call | tf_op jit(solution)/shard_map/pallas_call | solution.py:669
  482.1 7.1 convolution_convert_fusion.7.source
  489.2 12.9 %shard_map.207 = bf16[8,128,256]{2,1,0:T(8,128)(2,1)} custom-call(bf16[128,2048]{1,0:T(8,128)(2,1)} %convolution_convert_fusion.7.source), custom_call_target="tpu_custom_call" | custom-call | tf_op jit(solution)/shard_map/pallas_call | solution.py:669
  503.8 4.1 fusion.13
  507.9 4.7 multiply_convert_fusion
  515.2 4.9 convolution_convert_fusion.6
  520.2 5.1 convolution_convert_fusion.3
  525.2 55.4 %shard_map.208 = f32[128,2048]{1,0:T(8,128)} custom-call(bf16[8,128,2048]{2,1,0:T(8,128)(2,1)} %bitcast.158), custom_call_target="tpu_custom_call" | custom-call | tf_op jit(solution)/shard_map/pallas_call | solution.py:669
  585.7 5.6 convolution_convert_fusion.1
  591.2 170.3 %shard_map.209 = (bf16[8,64,768]{2,1,0:T(8,128)(2,1)}, bf16[8,64,2048]{2,1,0:T(8,128)(2,1)}, f32[4,64,2048]{2,1,0:T(8,128)}, f32[64,2048]{1,0:T(8,128)}, f32[8,128]{1,0:T(8,128)}) custom-call(bf16[4,8,64,768]{3,2,1,0:T(8,128)(2,1)} %bitcast.169, bf16[4,8,64,2048]{3,2,1,0:T(8,128)(2,1)} %bitcast.154, bf16[4,4,64,2048]{3,2,1,0:T(8,128)(2,1)} %bitcast.168, ...), custom_call_target="tpu_custom_call" | custom-call | tf_op jit(solution)/shard_map/pallas_call | solution.py:669
  770.8 4.5 reshape.448
  775.3 4.3 fusion.48
  (118 shorter events, 64.3 us)
Async XLA Ops:
  0.6 10.5 %copy-start.12 = (bf16[64,8192]{1,0:T(8,128)(2,1)S(1)}, bf16[64,8192]{1,0:T(8,128)(2,1)}, u32[]{:S(2)}) copy-start(bf16[64,8192]{1,0:T(8,128)(2,1)} %param.19) | copy-start | bytes 3145732
  2.0 1.3 copy-start.19
  8.2 4.3 copy-start.13
  217.5 5.4 copy-start.16
  217.5 5.4 copy-start.1
  223.0 1.9 copy-start.24
  224.8 4.7 copy-start.14
  232.7 3.2 copy-start
  232.7 21.3 %copy-start.2 = (bf16[1,128,2048]{2,1,0:T(8,128)(2,1)S(1)}, bf16[1,128,2048]{2,1,0:T(8,128)(2,1)}, u32[]{:S(2)}) copy-start(bf16[1,128,2048]{2,1,0:T(8,128)(2,1)} %param.12) | copy-start | bytes 1572868
  314.0 14.7 %copy-start.21 = (bf16[4,4,64,2048]{3,2,1,0:T(8,128)(2,1)S(1)}, bf16[4,4,64,2048]{3,2,1,0:T(8,128)(2,1)}, u32[]{:S(2)}) copy-start(bf16[4,4,64,2048]{3,2,1,0:T(8,128)(2,1)} %get-tuple-element.30) | copy-start | bytes 12582916
  314.0 14.7 %copy-start.22 = (bf16[8,128,2048]{2,1,0:T(8,128)(2,1)S(1)}, bf16[8,128,2048]{2,1,0:T(8,128)(2,1)}, u32[]{:S(2)}) copy-start(bf16[8,128,2048]{2,1,0:T(8,128)(2,1)} %get-tuple-element.29) | copy-start | bytes 12582916
  338.5 15.1 %copy-start.4 = (bf16[8,128,2048]{2,1,0:T(8,128)(2,1)S(1)}, bf16[8,128,2048]{2,1,0:T(8,128)(2,1)}, u32[]{:S(2)}) copy-start(bf16[8,128,2048]{2,1,0:T(8,128)(2,1)} %shard_map.205) | copy-start | bytes 12582916
  353.6 13.5 %copy-start.23 = (bf16[8,128,2048]{2,1,0:T(8,128)(2,1)S(1)}, bf16[8,128,2048]{2,1,0:T(8,128)(2,1)}, u32[]{:S(2)}) copy-start(bf16[8,128,2048]{2,1,0:T(8,128)(2,1)} %get-tuple-element.29) | copy-start | bytes 12582916
  379.5 99.9 %copy-start.7 = (bf16[1,128,2048]{2,1,0:T(8,128)(2,1)S(1)}, bf16[1,128,2048]{2,1,0:T(8,128)(2,1)}, u32[]{:S(2)}) copy-start(bf16[1,128,2048]{2,1,0:T(8,128)(2,1)} %param.23) | copy-start | bytes 1572868
  507.9 4.8 copy-start.11
  512.6 1.0 copy-start.9
  512.7 2.6 copy-start.5
  515.2 4.9 copy-start.25
  525.2 55.5 %copy-start.17 = (f32[2048]{0:T(1024)S(1)}, f32[2048]{0:T(1024)}, u32[]{:S(2)}) copy-start(f32[2048]{0:T(1024)} %copy-done.16) | copy-start | bytes 24580
  525.2 55.5 %copy-start.18 = (f32[128]{0:T(128)S(1)}, f32[128]{0:T(128)}, u32[]{:S(2)}) copy-start(f32[128]{0:T(128)} %fusion.42) | copy-start | bytes 1540
  525.2 57.1 %copy-start.20 = (f32[128]{0:T(128)S(1)}, f32[128]{0:T(128)}, u32[]{:S(2)}) copy-start(f32[128]{0:T(128)} %copy-done.19) | copy-start | bytes 1540
  525.2 60.4 %copy-start.3 = (bf16[128,2048]{1,0:T(8,128)(2,1)S(1)}, bf16[128,2048]{1,0:T(8,128)(2,1)}, u32[]{:S(2)}) copy-start(bf16[128,2048]{1,0:T(8,128)(2,1)} %shard_map.204) | copy-start | bytes 1572868
  766.9 3.8 copy-start.6
  782.3 4.4 copy-start.15
  (2 other events, 1.8 us)

commit v2 on v1

--- a/solution.py
+++ b/solution.py
@@ -842,117 +842,264 @@
     ).reshape(seqs * tokens, width)
 
 
-def reduce_kernel(rows, seqs, count, *refs):
-    p = Place(rows, seqs)
-    sources, targets = refs[:count], refs[count : 2 * count]
-    side, chain, sems = refs[2 * count :]
-    pool = Sems(sems)
-    greet(p.chain())
-    half = targets[0].shape[0] // 2
+def seq_reducers(place, pool, source, side, chain, target):
+    half = target.shape[0] // 2
     members = []
-    for number in range(count):
-        for c in range(2):
-            piece = pl.ds(c * half, half)
-            members.append(
-                SeqReduce(
-                    p,
-                    pool,
-                    lambda b, n=number, piece=piece: sources[n].at[b, piece],
-                    lambda b, n=number, piece=piece: side.at[n, b, piece],
-                    lambda w, b, n=number, piece=piece: chain.at[n, w, b, piece],
-                    targets[number].at[piece],
-                )
+    for c in range(2):
+        piece = pl.ds(c * half, half)
+        members.append(
+            SeqReduce(
+                place,
+                pool,
+                lambda b, piece=piece: source.at[b, piece],
+                lambda b, piece=piece: side.at[b, piece],
+                lambda w, b, piece=piece: chain.at[w, b, piece],
+                target.at[piece],
             )
-    for first in range(0, len(members), 2):
-        for t in range(p.n_hi):
-            for member in members[first : first + 2]:
-                member.start(t)
-    for first in range(0, len(members), 2):
-        for t in range(p.n_hi):
-            for member in members[first : first + 2]:
-                member.step(t)
-    for member in members:
+        )
+    return members
+
+
+def row_reducer(place, pool, source, core_slots, y_slots, target, add=add_into):
+    return RowReduce(
+        place,
+        pool,
+        source.shape[1],
+        lambda r, b: source.at[r, b],
+        lambda w, b: core_slots.at[w, b],
+        lambda b: y_slots.at[b],
+        lambda b: target.at[b],
+        add,
+    )
+
+
+def middle_kernel(
+    rows,
+    seqs,
+    h2,
+    out,
+    gu,
+    down,
+    h2_sum,
+    out_sum,
+    gu_sum,
+    down_sum,
+    h2_side,
+    h2_chain,
+    out_side,
+    out_chain,
+    gu_core,
+    gu_y,
+    down_core,
+    down_y,
+    sems,
+):
+    p, pool = Place(rows, seqs), Sems(sems)
+    greet(p.chain() + p.rows())
+    h2_parts = seq_reducers(p, pool, h2, h2_side, h2_chain, h2_sum)
+    out_parts = seq_reducers(p, pool, out, out_side, out_chain, out_sum)
+    gu_rows = row_reducer(p, pool, gu, gu_core, gu_y, gu_sum)
+    down_rows = row_reducer(p, pool, down, down_core, down_y, down_sum)
+    row_work = [(gu_rows, b) for b in range(gu_rows.blocks)] + [(down_rows, b) for b in range(down_rows.blocks)]
+    for t in range(p.n_hi):
+        for member in h2_parts:
+            member.start(t)
+    for member, block in row_work:
+        member.start(block)
+    for t in range(p.n_hi):
+        for member in out_parts:
+            member.start(t)
+    turns = [(member, t) for parts in (h2_parts, out_parts) for t in range(p.n_hi) for member in parts]
+    first = p.n_hi
+    share = -(-len(row_work) // first)
+    for number in range(first):
+        for member, t in turns[2 * number : 2 * number + 2]:
+            member.step(t)
+        for member, block in row_work[number * share : (number + 1) * share]:
+            member.step(block)
+    for member, t in turns[2 * first :]:
+        member.step(t)
+    for member, block in row_work:
+        member.close(block)
+    for member in h2_parts + out_parts + [gu_rows, down_rows]:
         member.finish()
 
 
-def reduced(rows, seqs, ident, sources):
-    count = len(sources)
-    tokens, width = sources[0].shape[0] // seqs, sources[0].shape[1]
-    sources = [source.reshape(seqs, tokens, width) for source in sources]
+def slots(array, copies=()):
+    return pltpu.VMEM(copies + array.shape[1:], array.dtype)
+
+
+def seq_slots(array):
+    half = array.shape[0] // 2
+    return [
+        pltpu.VMEM((half,) + array.shape[1:], array.dtype),
+        pltpu.VMEM((2, half) + array.shape[1:], array.dtype),
+    ]
+
+
+def row_slots(array):
+    return [slots(array, (2,)), slots(array)]
+
+
+def row_blocks(rows, array, count):
+    return array.reshape(rows, count, array.shape[0] // (rows * count), array.shape[1])
+
+
+def middle_sums(rows, seqs, h2, out, gu, down):
+    h2, out = (array.reshape(seqs, array.shape[0] // seqs, array.shape[1]) for array in (h2, out))
+    gu, down = row_blocks(rows, gu, seqs), row_blocks(rows, down, 4)
+    shapes = (
+        shape_of(h2.shape[1:], jnp.float32),
+        shape_of(out.shape[1:], jnp.float32),
+        shape_of(gu.shape[1:]),
+        shape_of(down.shape[1:]),
+    )
     return call(
-        functools.partial(reduce_kernel, rows, seqs, count),
-        (shape_of((tokens, width), jnp.float32),) * count,
-        ident,
-        sources,
-        [pltpu.VMEM] * count,
-        (pltpu.VMEM,) * count,
-        [
-            pltpu.VMEM((count, seqs // 2, tokens, width), jnp.bfloat16),
-            pltpu.VMEM((count, 2, seqs // 2, tokens, width), jnp.bfloat16),
-        ],
-        256,
+        functools.partial(middle_kernel, rows, seqs),
+        shapes,
+        4,
+        (h2, out, gu, down),
+        [pltpu.VMEM] * 4,
+        (pltpu.VMEM,) * 4,
+        seq_slots(h2) + seq_slots(out) + row_slots(gu) + row_slots(down),
+        320,
+    )
+
+
+class ColumnExchange:
+    def __init__(self, place, sems, piece, parts):
+        self.p, self.piece, self.parts = place, piece, parts
+        n = place.seq_count
+        self.own, self.send, self.recv = sems.take(1), sems.take(n), sems.take(n)
+
+    def start(self):
+        p, s = self.p, self.p.s
+        for step in range(p.seq_count):
+            t = p.peer(step)
+            piece = self.piece(t)
+            for offset, width, target in self.parts(s):
+                source = piece.at[:, pl.ds(offset, width)]
+                if step == 0:
+                    pltpu.make_async_copy(source, target, self.own(0)).start()
+                else:
+                    push(source, target, self.send(step), self.recv(s), (p.r, t))
+
+    def finish(self):
+        p = self.p
+        settle(self.piece(p.s), self.own(0))
+        for step in range(1, p.seq_count):
+            settle(self.piece(p.s), self.send(step))
+            settle(self.piece(p.s), self.recv(p.peer(step)))
+
+
+def late_kernel(
+    rows,
+    seqs,
+    hn,
+    out,
+    qkv,
+    gu,
+    hn_sum,
+    out_sum,
+    qkv_sum,
+    gate_got,
+    up_got,
+    hn_side,
+    hn_chain,
+    out_core,
+    out_y,
+    qkv_core,
+    qkv_y,
+    sems,
+):
+    p, pool = Place(rows, seqs), Sems(sems)
+    greet(p.peers() + p.rows())
+    hn_parts = seq_reducers(p, pool, hn, hn_side, hn_chain, hn_sum)
+    out_rows = row_reducer(p, pool, out, out_core, out_y, out_sum)
+    qkv_rows = row_reducer(p, pool, qkv, qkv_core, qkv_y, qkv_sum)
+    hidden_own = gu.shape[2] // 2
+    block = hidden_own // rows
+
+    def gu_parts(s):
+        for n, target in ((0, gate_got), (1, up_got)):
+            for r in range(rows):
+                yield n * hidden_own + r * block, block, columns(target, r * seqs + s, block)
+
+    swap = ColumnExchange(p, pool, lambda t: gu.at[t], gu_parts)
+    for t in range(p.n_hi):
+        for member in hn_parts:
+            member.start(t)
+    row_work = [(member, b) for member in (out_rows, qkv_rows) for b in range(member.blocks)]
+    for member, b in row_work:
+        member.start(b)
+    swap.start()
+    share = -(-len(row_work) // p.n_hi)
+    for t in range(p.n_hi):
+        for member in hn_parts:
+            member.step(t)
+        for member, b in row_work[t * share : (t + 1) * share]:
+            member.step(b)
+    for member, b in row_work:
+        member.close(b)
+    for member in hn_parts + [out_rows, qkv_rows, swap]:
+        member.finish()
+
+
+def late_sums(rows, seqs, hn, out, qkv, gu):
+    hn = hn.reshape(seqs, hn.shape[0] // seqs, hn.shape[1])
+    out, qkv = row_blocks(rows, out, seqs), row_blocks(rows, qkv, seqs)
+    got = shape_of((gu.shape[1], gu.shape[2] // 2 * seqs))
+    shapes = (
+        shape_of(hn.shape[1:], jnp.float32),
+        shape_of(out.shape[1:]),
+        shape_of(qkv.shape[1:]),
+        got,
+        got,
+    )
+    return call(
+        functools.partial(late_kernel, rows, seqs),
+        shapes,
+        6,
+        (hn, out, qkv, gu),
+        [pltpu.VMEM] * 4,
+        (pltpu.VMEM,) * 3 + (pl.ANY,) * 2,
+        seq_slots(hn) + row_slots(out) + row_slots(qkv),
+        320,
     )
 
 
 def closing_kernel(
     rows,
     seqs,
+    out,
     qkv,
-    gu,
-    down,
-    out,
     gain,
-    qkv_got,
-    gu_got,
-    down_sum,
     out_sum,
+    query_got,
+    key_got,
+    value_got,
     gain_sum,
-    qkv_core,
-    gu_core,
-    down_core,
-    out_core,
-    gain_core,
-    qkv_y,
-    gu_y,
-    down_y,
-    out_y,
-    gain_y,
     out_side,
     out_chain,
     gain_side,
     gain_chain,
+    gain_core,
+    gain_y,
     sems,
 ):
     p, pool = Place(rows, seqs), Sems(sems)
     greet(p.peers() + p.rows())
-
-    def over_rows(source, core_slots, y_slots, target, add=add_into):
-        return RowReduce(
-            p,
-            pool,
-            source.shape[1],
-            lambda r, b: source.at[r, b],
-            lambda w, b: core_slots.at[w, b],
-            lambda b: y_slots.at[b],
-            target,
-            add,
-        )
-
-    qkv_rows = over_rows(qkv, qkv_core, qkv_y, lambda b: qkv_y.at[b])
-    gu_rows = over_rows(gu, gu_core, gu_y, lambda b: gu_y.at[b])
-    down_rows = over_rows(down, down_core, down_y, lambda b: down_sum.at[b])
-    out_rows = over_rows(out, out_core, out_y, lambda b: out_y.at[b])
-    gain_rows = over_rows(gain, gain_core, gain_y, lambda b: gain_y.at[b], add_small)
-    qkv_swap = SeqExchange(p, pool, lambda t: qkv_y.at[t], lambda b: qkv_got.at[b])
-    gu_swap = SeqExchange(p, pool, lambda t: gu_y.at[t], lambda b: gu_got.at[b])
+    own_width = qkv.shape[2] // 3
+
+    def qkv_parts(s):
+        for n, target in enumerate((query_got, key_got, value_got)):
+            yield n * own_width, own_width, columns(target, s, own_width)
+
+    swap = ColumnExchange(p, pool, lambda t: qkv.at[t], qkv_parts)
     out_seq = SeqReduce(
-        p,
-        pool,
-        lambda b: out_y.at[b],
-        lambda b: out_side.at[b],
-        lambda w, b: out_chain.at[w, b],
-        out_sum,
-    )
+        p, pool, lambda b: out.at[b], lambda b: out_side.at[b], lambda w, b: out_chain.at[w, b], out_sum
+    )
+    gain_rows = row_reducer(p, pool, gain, gain_core, gain_y, gain_y, add_small)
     gain_seq = SeqReduce(
         p,
         pool,
@@ -962,71 +1109,37 @@
         gain_sum,
         add_small,
     )
-    members = (gain_rows, gu_rows, qkv_rows, out_rows, down_rows)
-    for member in members:
-        for block in range(member.blocks):
-            member.start(block)
-    for member in members:
-        for block in range(member.blocks):
-            member.step(block)
+    for block in range(seqs):
+        gain_rows.start(block)
+    for t in range(p.n_hi):
+        out_seq.start(t)
+    swap.start()
+    for block in range(seqs):
+        gain_rows.step(block)
     for block in range(seqs):
         gain_rows.close(block)
     for t in range(p.n_hi):
         gain_seq.start(t)
-    for block in range(seqs):
-        gu_rows.close(block)
-    gu_swap.start()
-    for block in range(seqs):
-        qkv_rows.close(block)
-    qkv_swap.start()
-    for block in range(seqs):
-        out_rows.close(block)
     for t in range(p.n_hi):
-        out_seq.start(t)
-    for block in range(down_rows.blocks):
-        down_rows.close(block)
-    for t in range(p.n_hi):
+        out_seq.step(t)
         gain_seq.step(t)
-        out_seq.step(t)
-    for step in range(1, seqs):
-        gu_swap.step(step)
-        qkv_swap.step(step)
-    for member in members + (gu_swap, qkv_swap, out_seq, gain_seq):
+    for member in (gain_rows, swap, out_seq, gain_seq):
         member.finish()
 
 
-def closing(rows, seqs, qkv, gu, down, out, gain):
-    def blocks_of(array, count):
-        return array.reshape(rows, count, array.shape[0] // (rows * count), array.shape[1])
-
-    qkv, gu, out, gain = (blocks_of(array, seqs) for array in (qkv, gu, out, gain))
-    down = blocks_of(down, 4)
-    args = (qkv, gu, down, out, gain)
-
-    def slots(array, copies):
-        return pltpu.VMEM(copies + array.shape[1:], array.dtype)
-
-    half = seqs // 2
-    shapes = (
-        shape_of(qkv.shape[1:]),
-        shape_of(gu.shape[1:]),
-        shape_of(down.shape[1:], jnp.float32),
-        shape_of(out.shape[2:], jnp.float32),
-        shape_of(gain.shape[2:], jnp.float32),
-    )
-    scratch = [slots(array, (2,)) for array in args] + [slots(array, ()) for array in args]
-    for array in (out, gain):
-        scratch.append(pltpu.VMEM((half,) + array.shape[2:], array.dtype))
-        scratch.append(pltpu.VMEM((2, half) + array.shape[2:], array.dtype))
+def closing(rows, seqs, out, qkv, gain):
+    gain = row_blocks(rows, gain, seqs)
+    got = shape_of((qkv.shape[1], qkv.shape[2] // 3 * seqs))
+    shapes = (shape_of(out.shape[1:]), got, got, got, shape_of(gain.shape[2:], jnp.float32))
     return call(
         functools.partial(closing_kernel, rows, seqs),
         shapes,
         9,
-        args,
-        [pltpu.VMEM] * 5,
-        (pl.ANY, pl.ANY, pltpu.VMEM, pltpu.VMEM, pltpu.VMEM),
-        scratch,
-        480,
+        (out, qkv, gain),
+        [pltpu.VMEM] * 3,
+        (pltpu.VMEM,) * 5,
+        seq_slots(out) + seq_slots(gain[0]) + row_slots(gain),
+        320,
     )
 
 
@@ -1119,7 +1232,7 @@
     h2_part = dot(gu_grad, wgu, 1, 1).astype(low)
     grad_down = dot(hidden, g_all, 0, 0).astype(low)
     grad_gu = dot(h2, gu_grad, 0, 0).astype(low)
-    h2_grad, out_sum = reduced(rows, seqs, 4, [h2_part, out_part])
+    h2_grad, out_sum, sum_gu, sum_down = middle_sums(rows, seqs, h2_part, out_part, grad_gu, grad_down)
     output = (middle + out_sum).astype(low)
 
     unused_two, second_back = jax.vjp(rms_norm, middle, gain_two)
@@ -1140,7 +1253,8 @@
         [member.reshape(row_tokens, own_width).astype(low) for member in (q_grad, k_grad, v_grad)], axis=1
     )
     grad_qkv = dot(hn, qkv_grad, 0, 0).astype(low)
-    (hn_grad,) = reduced(rows, seqs, 6, [dot(qkv_grad, wqkv, 1, 1).astype(low)])
+    hn_part = dot(qkv_grad, wqkv, 1, 1).astype(low)
+    hn_grad, sum_out, sum_qkv, got_gate, got_up = late_sums(rows, seqs, hn_part, grad_out, grad_qkv, sum_gu)
     unused_one, first_back = jax.vjp(rms_norm, residual, gain_one)
     residual_part, gain_one_grad = first_back(hn_grad)
     input_grad = middle_grad + residual_part
@@ -1149,27 +1263,18 @@
         [gain_one_grad.reshape(rows * seqs, deep), gain_two_grad.reshape(rows * seqs, deep)], axis=1
     )
     gain_grads = jnp.broadcast_to(gain_grads[:, None, :], (rows * seqs, 8, 2 * deep)).reshape(-1, 2 * deep)
-    got_qkv, got_gu, sum_down, sum_out, sum_gain = closing(
-        rows, seqs, grad_qkv, grad_gu, grad_down, grad_out, gain_grads
-    )
-    got_qkv = got_qkv.reshape(seqs, deep, 3, own_width).transpose(2, 1, 0, 3).reshape(3, deep, width).astype(f32)
-    got_gu = (
-        got_gu.reshape(seqs, deep, 2, rows, hidden_block)
-        .transpose(2, 1, 3, 0, 4)
-        .reshape(2, deep, w_gate.shape[1])
-        .astype(f32)
-    )
+    sum_out, got_query, got_key, got_value, sum_gain = closing(rows, seqs, sum_out, sum_qkv, gain_grads)
     return (
         output[None],
         input_grad[None],
-        got_qkv[0],
-        got_qkv[1],
-        got_qkv[2],
-        sum_out,
+        got_query.astype(f32),
+        got_key.astype(f32),
+        got_value.astype(f32),
+        sum_out.astype(f32),
         sum_gain[0, :deep],
-        got_gu[0],
-        got_gu[1],
-        sum_down.reshape(w_down.shape),
+        got_gate.astype(f32),
+        got_up.astype(f32),
+        sum_down.reshape(w_down.shape).astype(f32),
         sum_gain[0, deep:],
     )
 

time: 799 us -> 746 us (0.934)
  Pallas kernels: 606 us -> 565 us
  local copies, waits for them, and re-layouts: 43.5 us -> 17.8 us
  other arithmetic: 28.1 us -> 41.1 us
    pallas_call x7, Pallas kernels: 606 us -> 565 us  [call(): pl.pallas_call(kernel, out_shape=shapes, in_specs=[pl.BlockSpec(memory_sp...]
    convert_element_type x0 -> x7, other arithmetic: none -> 11.7 us  [the longest x1 1.78 us: split_local(): got_query.astype(f32)]
    slice x7 -> x0, local copies, waits for them, and re-layouts: 10.8 us -> none  [the longest x2 5.5 us: split_local(): got_gu[1]]
where the time goes in v2:
time: 746 us; the launch traced here: 738 us
  Pallas kernels  565 us (76%)
  matrix products  112 us (15%)
  other arithmetic  41.1 us (6%)
  local copies, waits for them, and re-layouts  17.8 us (2%)
    pallas_call x7, Pallas kernels, call(): pl.pallas_call(kernel, out_shape=shapes, in_specs=[pl.BlockSpec(memory_sp...  565 us
    dot_general x12, matrix products, dot(): lax.dot_general(left, right, (((left_axis,), (right_axis,)), ((), ())), p...  96.3 us

profile of v2, /device:TPU:0, one launch (start us, length us, event | category | flops | bytes accessed | tf_op | source)
XLA Modules:
  0.0 737.5 jit_solution(9151050982576944894)
XLA Ops:
  18.9 197.5 %shard_map.203 = (bf16[8,128,2048]{2,1,0:T(8,128)(2,1)}, bf16[8,128,2048]{2,1,0:T(8,128)(2,1)}, bf16[4,8,64,768]{3,2,1,0:T(8,128)(2,1)}, bf16[4,8,64,2048]{3,2,1...) custom-call(bf16[128,2048]{1,0:T(8,128)(2,1)} %bitcast.139, ...), custom_call_target="tpu_custom_call" | custom-call | tf_op jit(solution)/shard_map/pallas_call | solution.py:669
  217.4 3.1 multiply_reduce_fusion
  220.8 5.4 fusion.1
  228.1 3.6 convolution_convert_fusion.8
  232.8 3.3 divide_select_fusion
  240.6 16.8 %shard_map.204 = bf16[128,2048]{1,0:T(8,128)(2,1)} custom-call(bf16[8,128,256]{2,1,0:T(8,128)(2,1)} %copy.63.source), custom_call_target="tpu_custom_call" | custom-call | tf_op jit(solution)/shard_map/pallas_call | solution.py:669
  257.4 5.0 multiply_reduce_fusion.3
  263.4 54.1 %shard_map.205 = bf16[8,128,2048]{2,1,0:T(8,128)(2,1)} custom-call(bf16[128,2048]{1,0:T(8,128)(2,1)} %multiply_convert_fusion.4.source), custom_call_target="tpu_custom_call" | custom-call | tf_op jit(solution)/shard_map/pallas_call | solution.py:669
  317.5 14.7 %fusion.49 = f32[1024,2048]{0,1:T(8,128)} fusion(bf16[1024,2048]{1,0:T(8,128)(2,1)} %bitcast.147, bf16[2048,2048]{1,0:T(8,128)(2,1)} %bitcast.178), kind=kOutput, calls=%fused_computation.121 | convolution fusion | flops 8589934592 | bytes 20971520 | tf_op jit(solution)/shard_map/dot_general | solution.py:1147
  332.2 9.8 %fusion.4 = (bf16[1024,1024]{0,1:T(8,128)(2,1)}, bf16[1024,1024]{0,1:T(8,128)(2,1)}, bf16[1024,1024]{0,1:T(8,128)(2,1)S(1)}) fusion(f32[1024,2048]{0,1:T(8,128)} %fusion.49, bf16[1024,2048]{1,0:T(8,128)(2,1)S(1)} %bitcast.182, bf16[1024,2048]{1,0:T(8,128)(2,1)S(1)} %bitcast.180), kind=kOutput, calls=%fused_computation.12 | convolution fusion | flops 4311744512 | bytes 23068672 | tf_op jit(solution)/shard_map/dot_general | solution.py:1147
  342.0 14.8 %convolution_convert_fusion.2 = bf16[1024,2048]{1,0:T(8,128)(2,1)} fusion(bf16[2048,2048]{1,0:T(8,128)(2,1)} %bitcast.179, bf16[1024,1024]{0,1:T(8,128)(2,1)} %get-tuple-element.66, bf16[1024,1024]{0,1:T(8,128)(2,1)} %get-tuple-element.65), kind=kOutput, calls=%fused_computation.19 | convolution fusion | flops 8600420352 | bytes 16777216 | tf_op jit(solution)/shard_map/dot_general | solution.py:1147
  356.7 13.5 %convolution_convert_fusion = bf16[2048,2048]{1,0:T(8,128)(2,1)} fusion(bf16[1024,2048]{1,0:T(8,128)(2,1)S(1)} %bitcast.148, bf16[1024,1024]{0,1:T(8,128)(2,1)} %get-tuple-element.66, bf16[1024,1024]{0,1:T(8,128)(2,1)} %get-tuple-element.65), kind=kOutput, calls=%fused_computation.7 | convolution fusion | flops 8602517504 | bytes 16777216 | tf_op jit(solution)/shard_map/dot_general | solution.py:1147
  370.2 6.1 convolution_convert_fusion.4
  376.3 6.1 convolution_convert_fusion.5
  382.5 105.5 %shard_map.206 = (f32[128,2048]{1,0:T(8,128)}, f32[128,2048]{1,0:T(8,128)}, bf16[8,64,2048]{2,1,0:T(8,128)(2,1)}, bf16[4,64,2048]{2,1,0:T(8,128)(2,1)}) custom-call(bf16[8,128,2048]{2,1,0:T(8,128)(2,1)} %bitcast.144, bf16[8,128,2048]{2,1,0:T(8,128)(2,1)} %bitcast.146, bf16[4,8,64,2048]{3,2,1,0:T(8,128)(2,1)} %bitcast.140, bf16[4,4,64,2048]{3,2,1,0:T(8,128)(2,1)} %bitcast.145), custom_call_target="tpu_custom_call" | custom-call | tf_op jit(solution)/shard_map/pallas_call | solution.py:669
  492.1 7.1 convolution_convert_fusion.7.source
  499.2 15.0 %shard_map.207 = bf16[8,128,256]{2,1,0:T(8,128)(2,1)} custom-call(bf16[128,2048]{1,0:T(8,128)(2,1)} %convolution_convert_fusion.7.source), custom_call_target="tpu_custom_call" | custom-call | tf_op jit(solution)/shard_map/pallas_call | solution.py:669
  515.9 4.1 fusion.13
  520.0 4.7 multiply_convert_fusion
  527.3 4.9 convolution_convert_fusion.6
  532.2 5.2 convolution_convert_fusion.3
  539.1 5.6 convolution_convert_fusion.1
  544.7 101.9 %shard_map.208 = (f32[128,2048]{1,0:T(8,128)}, bf16[8,64,2048]{2,1,0:T(8,128)(2,1)}, bf16[8,64,768]{2,1,0:T(8,128)(2,1)}, bf16[64,8192]{1,0:T(8,128)(2,1)}, bf16[64,8192]{1,0:T(8,128)(2,1)}) custom-call(bf16[8,128,2048]{2,1,0:T(8,128)(2,1)} %bitcast.143, bf16[4,8,64,2048]{3,2,1,0:T(8,128)(2,1)} %bitcast.138, bf16[4,8,64,768]{3,2,1,0:T(8,128)(2,1)} %bitcast.154, ...), custom_call_target="tpu_custom_call" | custom-call | tf_op jit(solution)/shard_map/pallas_call | solution.py:669
  651.7 74.2 %shard_map.209 = (bf16[64,2048]{1,0:T(8,128)(2,1)}, bf16[64,2048]{1,0:T(8,128)(2,1)}, bf16[64,2048]{1,0:T(8,128)(2,1)}, bf16[64,2048]{1,0:T(8,128)(2,1)}, f32[8,128]{1,0:T(8,128)}) custom-call(bf16[8,64,2048]{2,1,0:T(8,128)(2,1)} %get-tuple-element.43.out, bf16[8,64,768]{2,1,0:T(8,128)(2,1)} %get-tuple-element.44.qkv, f32[4,8,8,128]{3,2,1,0:T(8,128)} %broadcast_in_dim.35.gain), custom_call_target="tpu_custom_call" | custom-call | tf_op jit(solution)/shard_map/pallas_call | solution.py:669
  (109 shorter events, 54.2 us)
Async XLA Ops:
  0.6 10.4 %copy-start.14 = (bf16[64,8192]{1,0:T(8,128)(2,1)S(1)}, bf16[64,8192]{1,0:T(8,128)(2,1)}, u32[]{:S(2)}) copy-start(bf16[64,8192]{1,0:T(8,128)(2,1)} %param.19) | copy-start | bytes 3145732
  2.0 3.4 copy-start.19
  220.8 5.4 copy-start.16
  220.8 5.4 copy-start.1
  226.2 1.9 copy-start.24
  228.1 4.7 copy-start.15
  236.1 3.2 copy-start
  236.1 21.3 %copy-start.2 = (bf16[1,128,2048]{2,1,0:T(8,128)(2,1)S(1)}, bf16[1,128,2048]{2,1,0:T(8,128)(2,1)}, u32[]{:S(2)}) copy-start(bf16[1,128,2048]{2,1,0:T(8,128)(2,1)} %param.12) | copy-start | bytes 1572868
  317.5 14.7 %copy-start.21 = (bf16[4,4,64,2048]{3,2,1,0:T(8,128)(2,1)S(1)}, bf16[4,4,64,2048]{3,2,1,0:T(8,128)(2,1)}, u32[]{:S(2)}) copy-start(bf16[4,4,64,2048]{3,2,1,0:T(8,128)(2,1)} %get-tuple-element.37) | copy-start | bytes 12582916
  317.5 14.7 %copy-start.22 = (bf16[8,128,2048]{2,1,0:T(8,128)(2,1)S(1)}, bf16[8,128,2048]{2,1,0:T(8,128)(2,1)}, u32[]{:S(2)}) copy-start(bf16[8,128,2048]{2,1,0:T(8,128)(2,1)} %get-tuple-element.36) | copy-start | bytes 12582916
  342.0 14.8 %copy-start.4 = (bf16[8,128,2048]{2,1,0:T(8,128)(2,1)S(1)}, bf16[8,128,2048]{2,1,0:T(8,128)(2,1)}, u32[]{:S(2)}) copy-start(bf16[8,128,2048]{2,1,0:T(8,128)(2,1)} %shard_map.205) | copy-start | bytes 12582916
  356.7 13.5 %copy-start.23 = (bf16[8,128,2048]{2,1,0:T(8,128)(2,1)S(1)}, bf16[8,128,2048]{2,1,0:T(8,128)(2,1)}, u32[]{:S(2)}) copy-start(bf16[8,128,2048]{2,1,0:T(8,128)(2,1)} %get-tuple-element.36) | copy-start | bytes 12582916
  382.5 107.0 %copy-start.6 = (bf16[1,128,2048]{2,1,0:T(8,128)(2,1)S(1)}, bf16[1,128,2048]{2,1,0:T(8,128)(2,1)}, u32[]{:S(2)}) copy-start(bf16[1,128,2048]{2,1,0:T(8,128)(2,1)} %param.23) | copy-start | bytes 1572868
  520.0 4.8 copy-start.10
  524.7 1.0 copy-start.8
  524.7 2.6 copy-start.5
  527.3 4.9 copy-start.25
  532.2 5.2 copy-start.11
  532.2 6.9 copy-start.3
  544.7 102.0 %copy-start.17 = (f32[2048]{0:T(1024)S(1)}, f32[2048]{0:T(1024)}, u32[]{:S(2)}) copy-start(f32[2048]{0:T(1024)} %copy-done.16) | copy-start | bytes 24580
  544.7 102.0 %copy-start.18 = (f32[128]{0:T(128)S(1)}, f32[128]{0:T(128)}, u32[]{:S(2)}) copy-start(f32[128]{0:T(128)} %fusion.42) | copy-start | bytes 1540
  544.7 103.6 %copy-start.20 = (f32[128]{0:T(128)S(1)}, f32[128]{0:T(128)}, u32[]{:S(2)}) copy-start(f32[128]{0:T(128)} %copy-done.19) | copy-start | bytes 1540
  648.3 86.1 %copy-start.13 = (bf16[64,8192]{1,0:T(8,128)(2,1)S(1)}, bf16[64,8192]{1,0:T(8,128)(2,1)}, u32[]{:S(2)}) copy-start(bf16[64,8192]{1,0:T(8,128)(2,1)} %get-tuple-element.50) | copy-start | bytes 3145732
  651.7 84.2 %copy-start.12 = (bf16[64,8192]{1,0:T(8,128)(2,1)S(1)}, bf16[64,8192]{1,0:T(8,128)(2,1)}, u32[]{:S(2)}) copy-start(bf16[64,8192]{1,0:T(8,128)(2,1)} %get-tuple-element.51) | copy-start | bytes 3145732
  (2 other events, 1.8 us)

commit v3 on v2

--- a/solution.py
+++ b/solution.py
@@ -309,7 +309,7 @@
 
 
 MESH = pl.DeviceIdType.MESH
-VMEM_BYTES = 60 * 1024 * 1024
+VMEM_BYTES = 62 * 1024 * 1024
 
 
 class Place:
@@ -992,154 +992,255 @@
             settle(self.piece(p.s), self.recv(p.peer(step)))
 
 
-def late_kernel(
+def nt(left, right):
+    return lax.dot_general(left, right, (((1,), (1,)), ((), ())), preferred_element_type=jnp.float32)
+
+
+def tn(left, right):
+    return lax.dot_general(left, right, (((0,), (0,)), ((), ())), preferred_element_type=jnp.float32)
+
+
+def nn(left, right):
+    return lax.dot_general(left, right, (((1,), (0,)), ((), ())), preferred_element_type=jnp.float32)
+
+
+def attention_back(qkv, do, dqkv, key_place, query_low, query_high, shift, dq_turned, head_size):
+    tokens, own_width = do.shape
+    scale = head_size ** (-0.5)
+    keys_step = 256
+    for head in range(own_width // head_size):
+        lanes = pl.ds(head * head_size, head_size)
+        key_lanes = pl.ds(own_width + head * head_size, head_size)
+        value_lanes = pl.ds(2 * own_width + head * head_size, head_size)
+        dq_turned[...] = jnp.zeros_like(dq_turned)
+
+        @pl.loop(0, tokens // keys_step)
+        def _(step):
+            rows = pl.ds(pl.multiple_of(step * keys_step, keys_step), keys_step)
+            key, value = qkv[rows, key_lanes], qkv[rows, value_lanes]
+            queries, grads = qkv[:, lanes], do[:, lanes]
+            places = key_place[rows, :]
+            allowed = (places >= query_low[...]) & (places <= query_high[...])
+            scores = nt(key, queries) * scale - shift[...]
+            sig = jnp.where(allowed, jax.nn.sigmoid(scores), 0.0)
+            score_grad = (nt(value, grads) * sig * (1.0 - sig)).astype(jnp.bfloat16)
+            dqkv[rows, value_lanes] = nn(sig.astype(jnp.bfloat16), grads).astype(jnp.bfloat16)
+            dqkv[rows, key_lanes] = (nn(score_grad, queries) * scale).astype(jnp.bfloat16)
+            dq_turned[...] += nn(key.T, score_grad)
+
+        dqkv[:, lanes] = (dq_turned[...].T * scale).astype(jnp.bfloat16)
+
+
+def back_kernel(
     rows,
     seqs,
+    head_size,
+    do_own,
+    qkv,
     hn,
+    wqkv,
     out,
-    qkv,
     gu,
+    gain_two_part,
+    gain_one,
+    key_place,
+    query_low,
+    query_high,
+    shift,
     hn_sum,
-    out_sum,
-    qkv_sum,
-    gate_got,
-    up_got,
-    hn_side,
-    hn_chain,
-    out_core,
-    out_y,
-    qkv_core,
-    qkv_y,
-    sems,
-):
-    p, pool = Place(rows, seqs), Sems(sems)
-    greet(p.peers() + p.rows())
-    hn_parts = seq_reducers(p, pool, hn, hn_side, hn_chain, hn_sum)
-    out_rows = row_reducer(p, pool, out, out_core, out_y, out_sum)
-    qkv_rows = row_reducer(p, pool, qkv, qkv_core, qkv_y, qkv_sum)
-    hidden_own = gu.shape[2] // 2
-    block = hidden_own // rows
-
-    def gu_parts(s):
-        for n, target in ((0, gate_got), (1, up_got)):
-            for r in range(rows):
-                yield n * hidden_own + r * block, block, columns(target, r * seqs + s, block)
-
-    swap = ColumnExchange(p, pool, lambda t: gu.at[t], gu_parts)
-    for t in range(p.n_hi):
-        for member in hn_parts:
-            member.start(t)
-    row_work = [(member, b) for member in (out_rows, qkv_rows) for b in range(member.blocks)]
-    for member, b in row_work:
-        member.start(b)
-    swap.start()
-    share = -(-len(row_work) // p.n_hi)
-    for t in range(p.n_hi):
-        for member in hn_parts:
-            member.step(t)
-        for member, b in row_work[t * share : (t + 1) * share]:
-            member.step(b)
-    for member, b in row_work:
-        member.close(b)
-    for member in hn_parts + [out_rows, qkv_rows, swap]:
-        member.finish()
-
-
-def late_sums(rows, seqs, hn, out, qkv, gu):
-    hn = hn.reshape(seqs, hn.shape[0] // seqs, hn.shape[1])
-    out, qkv = row_blocks(rows, out, seqs), row_blocks(rows, qkv, seqs)
-    got = shape_of((gu.shape[1], gu.shape[2] // 2 * seqs))
-    shapes = (
-        shape_of(hn.shape[1:], jnp.float32),
-        shape_of(out.shape[1:]),
-        shape_of(qkv.shape[1:]),
-        got,
-        got,
-    )
-    return call(
-        functools.partial(late_kernel, rows, seqs),
-        shapes,
-        6,
-        (hn, out, qkv, gu),
-        [pltpu.VMEM] * 4,
-        (pltpu.VMEM,) * 3 + (pl.ANY,) * 2,
-        seq_slots(hn) + row_slots(out) + row_slots(qkv),
-        320,
-    )
-
-
-def closing_kernel(
-    rows,
-    seqs,
-    out,
-    qkv,
-    gain,
     out_sum,
     query_got,
     key_got,
     value_got,
-    gain_sum,
+    gate_got,
+    up_got,
+    gain_got,
+    do,
+    dqkv,
+    dq_turned,
+    hn_part,
+    hn_side,
+    hn_chain,
+    grad_qkv,
+    qkv_core,
+    qkv_y,
+    out_core,
+    out_y,
     out_side,
     out_chain,
-    gain_side,
-    gain_chain,
+    gains,
     gain_core,
     gain_y,
     sems,
 ):
     p, pool = Place(rows, seqs), Sems(sems)
     greet(p.peers() + p.rows())
-    own_width = qkv.shape[2] // 3
+    tokens, own_width = do.shape
+    block_tokens = tokens // seqs
+    width = wqkv.shape[0]
+
+    def block_rows(b):
+        return pl.ds(pl.multiple_of(b * block_tokens, block_tokens), block_tokens)
+
+    do_swap = SeqExchange(
+        p, pool, lambda t: columns(do_own, t, own_width), lambda b: do.at[block_rows(b), :]
+    )
+    do_swap.start()
+    out_rows = row_reducer(p, pool, out, out_core, out_y, out_y)
+    for b in range(seqs):
+        out_rows.start(b)
+    hidden_own = gu.shape[2] // 2
+    block = hidden_own // rows
+
+    def gu_parts(s):
+        for n, target in ((0, gate_got), (1, up_got)):
+            for r in range(rows):
+                yield n * hidden_own + r * block, block, columns(target, r * seqs + s, block)
+
+    gu_swap = ColumnExchange(p, pool, lambda t: gu.at[t], gu_parts)
 
     def qkv_parts(s):
         for n, target in enumerate((query_got, key_got, value_got)):
             yield n * own_width, own_width, columns(target, s, own_width)
 
-    swap = ColumnExchange(p, pool, lambda t: qkv.at[t], qkv_parts)
+    qkv_swap = ColumnExchange(p, pool, lambda t: qkv_y.at[t], qkv_parts)
+    qkv_rows = row_reducer(p, pool, grad_qkv, qkv_core, qkv_y, qkv_y)
+    hn_parts = seq_reducers(p, pool, hn_part, hn_side, hn_chain, hn_sum)
     out_seq = SeqReduce(
-        p, pool, lambda b: out.at[b], lambda b: out_side.at[b], lambda w, b: out_chain.at[w, b], out_sum
-    )
-    gain_rows = row_reducer(p, pool, gain, gain_core, gain_y, gain_y, add_small)
-    gain_seq = SeqReduce(
+        p, pool, lambda b: out_y.at[b], lambda b: out_side.at[b], lambda w, b: out_chain.at[w, b], out_sum
+    )
+    quarter = width // rows
+    gain_rows = RowReduce(
         p,
         pool,
-        lambda b: gain_y.at[b],
-        lambda b: gain_side.at[b],
-        lambda w, b: gain_chain.at[w, b],
-        gain_sum,
+        1,
+        lambda r, b: columns(gains, r, quarter),
+        lambda w, b: gain_core.at[w],
+        lambda b: gain_y,
+        lambda b: gain_y,
         add_small,
     )
-    for block in range(seqs):
-        gain_rows.start(block)
+    gain_width = 2 * quarter // seqs
+    gain_swap = SeqExchange(
+        p, pool, lambda t: columns(gain_y, t // 2, gain_width), lambda b: gain_got.at[b]
+    )
+
+    for step in range(1, seqs):
+        do_swap.step(step)
+    settle(do.at[block_rows(p.s), :], do_swap.own(0))
+    gu_swap.start()
+    for b in range(seqs):
+        out_rows.step(b)
+    attention_back(qkv, do, dqkv, key_place, query_low, query_high, shift, dq_turned, head_size)
+
+    gains[0:8, :] = jnp.zeros_like(gains[0:8, :])
+    gains[8:16, :] = gain_two_part[...]
+    column_step = 512
     for t in range(p.n_hi):
-        out_seq.start(t)
-    swap.start()
-    for block in range(seqs):
-        gain_rows.step(block)
-    for block in range(seqs):
-        gain_rows.close(block)
+        pair = hn_parts[0].turn(t)
+        tall = pl.ds(pl.multiple_of(pair * 2 * block_tokens, 2 * block_tokens), 2 * block_tokens)
+
+        @pl.loop(0, width // column_step)
+        def _(c):
+            lanes = pl.ds(pl.multiple_of(c * column_step, column_step), column_step)
+            part = nt(dqkv[tall, :], wqkv[lanes, :])
+            hn_part[2 * pair, :, lanes] = part[:block_tokens].astype(jnp.bfloat16)
+            hn_part[2 * pair + 1, :, lanes] = part[block_tokens:].astype(jnp.bfloat16)
+            terms = part * hn[tall, lanes].astype(jnp.float32)
+            gains[0:8, lanes] += jnp.sum(terms.reshape(-1, 8, column_step), axis=0)
+
+        for member in hn_parts:
+            member.start(t)
+    gains[0:8, :] = gains[0:8, :] / gain_one[...]
+    gain_rows.start(0)
+
+    @pl.loop(0, width // 256)
+    def _(c):
+        lanes = pl.ds(pl.multiple_of(c * 256, 256), 256)
+        total = tn(hn[:, lanes], dqkv[...]).astype(jnp.bfloat16)
+        piece = total.reshape((4,) + (total.shape[0] // 4, total.shape[1]))
+        for n in range(4):
+            grad_qkv[c * 4 // seqs, lax.rem(c * 4, seqs) + n] = piece[n]
+
+    for b in range(seqs):
+        qkv_rows.start(b)
+    gain_rows.step(0)
     for t in range(p.n_hi):
-        gain_seq.start(t)
+        for member in hn_parts:
+            member.step(t)
+        if t == 0:
+            for b in range(seqs):
+                qkv_rows.step(b)
+            gain_rows.close(0)
+            gain_swap.start()
+        if t == 1:
+            for b in range(seqs):
+                out_rows.close(b)
+            for k in range(p.n_hi):
+                out_seq.start(k)
+        if t == 2:
+            for b in range(seqs):
+                qkv_rows.close(b)
+            qkv_swap.start()
     for t in range(p.n_hi):
         out_seq.step(t)
-        gain_seq.step(t)
-    for member in (gain_rows, swap, out_seq, gain_seq):
+    for step in range(1, seqs):
+        gain_swap.step(step)
+        settle(do.at[block_rows(p.s), :], do_swap.send(step))
+    for member in hn_parts + [out_rows, qkv_rows, gain_rows, gu_swap, qkv_swap, out_seq, gain_swap]:
         member.finish()
 
 
-def closing(rows, seqs, out, qkv, gain):
-    gain = row_blocks(rows, gain, seqs)
-    got = shape_of((qkv.shape[1], qkv.shape[2] // 3 * seqs))
-    shapes = (shape_of(out.shape[1:]), got, got, got, shape_of(gain.shape[2:], jnp.float32))
+def back(rows, seqs, head_size, do_own, qkv, hn, wqkv, out, gu, gain_two_part, gain_one, meta):
+    tokens, own_width = qkv.shape[0], qkv.shape[1] // 3
+    width = hn.shape[1]
+    low = jnp.bfloat16
+    out = row_blocks(rows, out, seqs)
+    block_tokens = tokens // seqs
+    hn_dims, qkv_dims = (seqs, block_tokens, width), (rows, seqs, width // (rows * seqs), 3 * own_width)
+    deep = width // (rows * seqs)
+    quarter = width // rows
+    got = shape_of((deep, width))
+    gu_got = shape_of((deep, gu.shape[2] // 2 * seqs))
+    gain_width = 2 * quarter // seqs
+    shapes = (
+        shape_of(hn_dims[1:], jnp.float32),
+        shape_of(out.shape[2:]),
+        got,
+        got,
+        got,
+        gu_got,
+        gu_got,
+        shape_of((seqs, 16, gain_width), jnp.float32),
+    )
+    hn_like, qkv_like, out_like = shape_of(hn_dims), shape_of(qkv_dims), shape_of(out.shape)
+    scratch = (
+        [
+            pltpu.VMEM((tokens, own_width), low),
+            pltpu.VMEM(qkv.shape, low),
+            pltpu.VMEM((head_size, tokens), jnp.float32),
+            pltpu.VMEM(hn_dims, low),
+        ]
+        + seq_slots(hn_like)
+        + [pltpu.VMEM(qkv_dims, low)]
+        + row_slots(qkv_like)
+        + row_slots(out_like)
+        + seq_slots(shape_of(out.shape[1:]))
+        + [
+            pltpu.VMEM((16, width), jnp.float32),
+            pltpu.VMEM((2, 16, quarter), jnp.float32),
+            pltpu.VMEM((16, quarter), jnp.float32),
+        ]
+    )
     return call(
-        functools.partial(closing_kernel, rows, seqs),
+        functools.partial(back_kernel, rows, seqs, head_size),
         shapes,
-        9,
-        (out, qkv, gain),
-        [pltpu.VMEM] * 3,
-        (pltpu.VMEM,) * 5,
-        seq_slots(out) + seq_slots(gain[0]) + row_slots(gain),
-        320,
+        6,
+        (do_own, qkv, hn, wqkv, out, gu, gain_two_part, gain_one) + meta,
+        [pltpu.VMEM] * 12,
+        (pltpu.VMEM,) * 5 + (pl.ANY,) * 2 + (pltpu.VMEM,),
+        scratch,
+        480,
     )
 
 
@@ -1235,35 +1336,36 @@
     h2_grad, out_sum, sum_gu, sum_down = middle_sums(rows, seqs, h2_part, out_part, grad_gu, grad_down)
     output = (middle + out_sum).astype(low)
 
-    unused_two, second_back = jax.vjp(rms_norm, middle, gain_two)
-    middle_part, gain_two_grad = second_back(h2_grad)
-    middle_grad = g_low.astype(f32) + middle_part
+    inverse = lax.rsqrt(jnp.mean(middle * middle, axis=-1, keepdims=True) + EPSILON)
+    scaled_grad = gain_two * h2_grad
+    gain_two_part = jnp.sum((h2_grad * middle * inverse).reshape(-1, 8, width), axis=0)
+    middle_grad = (
+        g_low.astype(f32)
+        + inverse * scaled_grad
+        - middle * inverse**3 * jnp.mean(scaled_grad * middle, axis=-1, keepdims=True)
+    )
     branch = middle_grad.astype(low)
     grad_out = dot(attended, branch, 0, 0).astype(low)
-    o_grad = to_heads(rows, seqs, 5, dot(branch, wout, 1, 1).astype(low))
-    o_grad = o_grad.reshape(row_tokens, heads_own, head_size)
-
-    sig = sigmoids()
-    slopes = jnp.einsum("qhd,khd->hqk", o_grad, values, preferred_element_type=f32)
-    score_grad = (slopes * sig * (1.0 - sig)).astype(low)
-    q_grad = jnp.einsum("hqk,khd->qhd", score_grad, keys, preferred_element_type=f32) * scale
-    k_grad = jnp.einsum("hqk,qhd->khd", score_grad, queries, preferred_element_type=f32) * scale
-    v_grad = jnp.einsum("hqk,qhd->khd", sig.astype(low), o_grad, preferred_element_type=f32)
-    qkv_grad = jnp.concatenate(
-        [member.reshape(row_tokens, own_width).astype(low) for member in (q_grad, k_grad, v_grad)], axis=1
-    )
-    grad_qkv = dot(hn, qkv_grad, 0, 0).astype(low)
-    hn_part = dot(qkv_grad, wqkv, 1, 1).astype(low)
-    hn_grad, sum_out, sum_qkv, got_gate, got_up = late_sums(rows, seqs, hn_part, grad_out, grad_qkv, sum_gu)
-    unused_one, first_back = jax.vjp(rms_norm, residual, gain_one)
-    residual_part, gain_one_grad = first_back(hn_grad)
-    input_grad = middle_grad + residual_part
-
-    gain_grads = jnp.concatenate(
-        [gain_one_grad.reshape(rows * seqs, deep), gain_two_grad.reshape(rows * seqs, deep)], axis=1
-    )
-    gain_grads = jnp.broadcast_to(gain_grads[:, None, :], (rows * seqs, 8, 2 * deep)).reshape(-1, 2 * deep)
-    sum_out, got_query, got_key, got_value, sum_gain = closing(rows, seqs, sum_out, sum_qkv, gain_grads)
+    do_own = dot(branch, wout, 1, 1).astype(low)
+    place = segment * row_tokens + position
+    back_meta = (
+        place[:, None],
+        (segment * row_tokens)[None, :],
+        place[None, :],
+        jnp.log(length_of.astype(f32))[None, :],
+    )
+    hn_grad, sum_out, got_query, got_key, got_value, got_gate, got_up, got_gain = back(
+        rows, seqs, head_size, do_own, qkv, hn, wqkv, grad_out, sum_gu, gain_two_part, gain_one[None, :], back_meta
+    )
+    spread_inverse = lax.rsqrt(jnp.mean(residual * residual, axis=-1, keepdims=True) + EPSILON)
+    scaled_grad = gain_one * hn_grad
+    input_grad = (
+        middle_grad
+        + spread_inverse * scaled_grad
+        - residual * spread_inverse**3 * jnp.mean(scaled_grad * residual, axis=-1, keepdims=True)
+    )
+    gain_sums = jnp.sum(got_gain, axis=0).reshape(2, 8, 2, deep).sum(axis=1)
+    gain_sums = lax.dynamic_index_in_dim(gain_sums, lax.rem(lax.axis_index("seq"), 2), 1, keepdims=False)
     return (
         output[None],
         input_grad[None],
@@ -1271,11 +1373,11 @@
         got_key.astype(f32),
         got_value.astype(f32),
         sum_out.astype(f32),
-        sum_gain[0, :deep],
+        gain_sums[0],
         got_gate.astype(f32),
         got_up.astype(f32),
         sum_down.reshape(w_down.shape).astype(f32),
-        sum_gain[0, deep:],
+        gain_sums[1],
     )
 
 

time: 746 us -> 650 us (0.87)
  Pallas kernels: 565 us -> 506 us
  matrix products: 112 us -> 85.2 us
  other arithmetic: 41.1 us -> 33.5 us
    pallas_call x7 -> x5, Pallas kernels: 565 us -> 506 us  [call(): pl.pallas_call(kernel, out_shape=shapes, in_specs=[pl.BlockSpec(memory_sp...]
    dot_general x12 -> x10, matrix products: 96.3 us -> 80.1 us  [dot(): lax.dot_general(left, right, (((left_axis,), (right_axis,)), ((), ())), p...]
    dot_general x5 -> x0, matrix products: 14.4 us -> none  [the longest x1 4.73 us: split_local(): jnp.einsum('qhd,khd->hqk', o_grad, values, preferred_element_type=f32)]
where the time goes in v3:
time: 650 us; the launch traced here: 641 us
  Pallas kernels  506 us (78%)
  matrix products  85.2 us (13%)
  other arithmetic  33.5 us (5%)
  local copies, waits for them, and re-layouts  14.9 us (2%)
    pallas_call x5, Pallas kernels, call(): pl.pallas_call(kernel, out_shape=shapes, in_specs=[pl.BlockSpec(memory_sp...  506 us
    dot_general x10, matrix products, dot(): lax.dot_general(left, right, (((left_axis,), (right_axis,)), ((), ())), p...  80.1 us

profile of v3, /device:TPU:0, one launch (start us, length us, event | category | flops | bytes accessed | tf_op | source)
XLA Modules:
  0.0 641.2 jit_solution(4787938354456096569)
XLA Ops:
  7.9 1.5 pad_maximum_fusion.3.wgu
  10.1 197.5 %shard_map.203 = (bf16[8,128,2048]{2,1,0:T(8,128)(2,1)}, bf16[8,128,2048]{2,1,0:T(8,128)(2,1)}, bf16[4,8,64,768]{3,2,1,0:T(8,128)(2,1)}, bf16[4,8,64,2048]{3,2,1...) custom-call(bf16[128,2048]{1,0:T(8,128)(2,1)} %bitcast.143, ...), custom_call_target="tpu_custom_call" | custom-call | tf_op jit(solution)/shard_map/pallas_call | solution.py:669
  208.8 3.2 multiply_reduce_fusion
  214.1 3.4 convolution_convert_fusion.6.qkv
  220.4 1.5 compare_and_fusion
  222.0 5.1 fusion.9
  228.4 16.8 %shard_map.204 = bf16[128,2048]{1,0:T(8,128)(2,1)} custom-call(bf16[8,128,256]{2,1,0:T(8,128)(2,1)} %copy.111.source), custom_call_target="tpu_custom_call" | custom-call | tf_op jit(solution)/shard_map/pallas_call | solution.py:669
  245.2 5.0 multiply_reduce_fusion.2
  251.2 54.1 %shard_map.205 = bf16[8,128,2048]{2,1,0:T(8,128)(2,1)} custom-call(bf16[128,2048]{1,0:T(8,128)(2,1)} %multiply_convert_fusion.3.source), custom_call_target="tpu_custom_call" | custom-call | tf_op jit(solution)/shard_map/pallas_call | solution.py:669
  305.4 14.7 %fusion.60 = f32[1024,2048]{0,1:T(8,128)} fusion(bf16[1024,2048]{1,0:T(8,128)(2,1)} %bitcast.147, bf16[2048,2048]{1,0:T(8,128)(2,1)} %bitcast.180), kind=kOutput, calls=%fused_computation.137 | convolution fusion | flops 8589934592 | bytes 20971520 | tf_op jit(solution)/shard_map/dot_general | solution.py:1248
  320.1 9.7 %fusion.4 = (bf16[1024,1024]{0,1:T(8,128)(2,1)}, bf16[1024,1024]{0,1:T(8,128)(2,1)}, bf16[1024,1024]{0,1:T(8,128)(2,1)S(1)}) fusion(f32[1024,2048]{0,1:T(8,128)} %fusion.60, bf16[1024,2048]{1,0:T(8,128)(2,1)S(1)} %bitcast.186, bf16[1024,2048]{1,0:T(8,128)(2,1)S(1)} %bitcast.184), kind=kOutput, calls=%fused_computation.11 | convolution fusion | flops 4311744512 | bytes 23068672 | tf_op jit(solution)/shard_map/dot_general | solution.py:1248
  329.8 6.1 convolution_convert_fusion.3
  335.9 13.7 %convolution_convert_fusion = bf16[2048,2048]{1,0:T(8,128)(2,1)} fusion(bf16[1024,2048]{1,0:T(8,128)(2,1)S(1)} %bitcast.148, bf16[1024,1024]{0,1:T(8,128)(2,1)} %get-tuple-element.58, bf16[1024,1024]{0,1:T(8,128)(2,1)} %get-tuple-element.57), kind=kOutput, calls=%fused_computation.6 | convolution fusion | flops 8602517504 | bytes 16777216 | tf_op jit(solution)/shard_map/dot_general | solution.py:1248
  349.5 6.2 convolution_convert_fusion.4
  355.8 12.0 %convolution_convert_fusion.2 = bf16[1024,2048]{1,0:T(8,128)(2,1)} fusion(bf16[2048,2048]{1,0:T(8,128)(2,1)S(1)} %bitcast.183, bf16[1024,1024]{0,1:T(8,128)(2,1)} %get-tuple-element.58, bf16[1024,1024]{0,1:T(8,128)(2,1)} %get-tuple-element.57), kind=kOutput, calls=%fused_computation.19 | convolution fusion | flops 8600420352 | bytes 16777216 | tf_op jit(solution)/shard_map/dot_general | solution.py:1248
  367.8 105.1 %shard_map.206 = (f32[128,2048]{1,0:T(8,128)}, f32[128,2048]{1,0:T(8,128)}, bf16[8,64,2048]{2,1,0:T(8,128)(2,1)}, bf16[4,64,2048]{2,1,0:T(8,128)(2,1)}) custom-call(bf16[8,128,2048]{2,1,0:T(8,128)(2,1)} %bitcast.146, bf16[8,128,2048]{2,1,0:T(8,128)(2,1)} %bitcast.145, bf16[4,8,64,2048]{3,2,1,0:T(8,128)(2,1)} %bitcast.142, bf16[4,4,64,2048]{3,2,1,0:T(8,128)(2,1)} %bitcast.144), custom_call_target="tpu_custom_call" | custom-call | tf_op jit(solution)/shard_map/pallas_call | solution.py:669
  473.0 2.2 bitcast_reduce_fusion.gain_two_part
  477.9 5.6 convolution_convert_fusion.1
  483.5 3.7 convolution_convert_fusion.5.do_own
  489.6 5.1 fusion.1.hn
  495.4 132.4 %shard_map.207 = (f32[128,2048]{1,0:T(8,128)}, bf16[64,2048]{1,0:T(8,128)(2,1)}, bf16[64,2048]{1,0:T(8,128)(2,1)}, bf16[64,2048]{1,0:T(8,128)(2,1)}, bf16[64,204...) custom-call(bf16[128,2048]{1,0:T(8,128)(2,1)} %convolution_convert_fusion.5.do_own, ...), custom_call_target="tpu_custom_call" | custom-call | tf_op jit(solution)/shard_map/pallas_call | solution.py:669
  627.9 2.8 convert_element_type.154
  630.7 2.7 convert_element_type.155
  639.1 1.6 bitcast_convert_fusion
  (114 shorter events, 27.7 us)
Async XLA Ops:
  1.7 4.7 copy-start.12
  208.8 3.5 copy-start
  220.4 267.4 %copy-start.18 = (s32[1024]{0:T(1024)}, s32[1024]{0:T(1024)S(1)}, u32[]{:S(2)}) copy-start(s32[1024]{0:T(1024)S(1)} %get-tuple-element.80) | copy-start | bytes 12292
  222.0 5.2 copy-start.20
  222.0 23.2 %copy-start.5 = (bf16[1,128,2048]{2,1,0:T(8,128)(2,1)S(1)}, bf16[1,128,2048]{2,1,0:T(8,128)(2,1)}, u32[]{:S(2)}) copy-start(bf16[1,128,2048]{2,1,0:T(8,128)(2,1)} %param.12) | copy-start | bytes 1572868
  305.3 14.7 %copy-start.22 = (bf16[4,4,64,2048]{3,2,1,0:T(8,128)(2,1)S(1)}, bf16[4,4,64,2048]{3,2,1,0:T(8,128)(2,1)}, u32[]{:S(2)}) copy-start(bf16[4,4,64,2048]{3,2,1,0:T(8,128)(2,1)} %get-tuple-element.35) | copy-start | bytes 12582916
  305.4 14.7 %copy-start.23 = (bf16[8,128,2048]{2,1,0:T(8,128)(2,1)S(1)}, bf16[8,128,2048]{2,1,0:T(8,128)(2,1)}, u32[]{:S(2)}) copy-start(bf16[8,128,2048]{2,1,0:T(8,128)(2,1)} %get-tuple-element.34) | copy-start | bytes 12582916
  329.8 6.1 copy-start.8
  329.8 26.0 %slice-start.2 = ((s8[8388608]{0:T(1024)(128)(4,1)}), s8[4194304]{0:T(1024)(128)(4,1)S(1)}, s32[]{:S(2)}) async-start(s8[8388608]{0:T(1024)(128)(4,1)} %bitcast.181), calls=%async_computation.2 | async-start | bytes 8388608
  335.9 19.9 %slice-start.3 = ((s8[8388608]{0:T(1024)(128)(4,1)}), s8[4194304]{0:T(1024)(128)(4,1)S(1)}, s32[]{:S(2)}) async-start(s8[8388608]{0:T(1024)(128)(4,1)} %bitcast.181), calls=%async_computation.3 | async-start | bytes 8388608
  472.9 3.7 copy-start.3
  472.9 3.7 copy-start.10
  473.0 3.7 copy-start.13
  476.6 6.9 %slice-start = ((s8[8388608]{0:T(1024)(128)(4,1)}), s8[4194304]{0:T(1024)(128)(4,1)S(1)}, s32[]{:S(2)}) async-start(s8[8388608]{0:T(1024)(128)(4,1)} %bitcast.138), calls=%async_computation | async-start | bytes 8388608
  477.9 5.6 copy-start.1
  477.9 5.6 slice-start.1
  627.8 5.6 copy-start.7
  627.8 5.9 copy-start.2
  630.7 4.4 copy-start.17
  630.7 5.3 copy-start.16
  633.4 3.4 copy-start.15
  633.4 4.2 copy-start.14
  633.4 5.0 copy-start.19
  633.4 5.7 copy-start.11
  (6 other events, 12.6 us)

commit v4 on v3

--- a/solution.py
+++ b/solution.py
@@ -387,6 +387,7 @@
 class SeqGather:
     def __init__(self, place, sems, source, at, arrived=no_op):
         self.p, self.source, self.at, self.arrived = place, source, at, arrived
+        self.own_done = False
         n = place.n_hi
         self.own, self.up, self.down = sems.take(1), sems.take(n), sems.take(n)
         self.side, self.recv = sems.take(n), sems.take(2 * n)
@@ -452,9 +453,14 @@
             settle(self.at(block), self.recv(block))
             self.arrived(block)
 
+    def settle_own(self):
+        settle(self.at(self.p.s), self.own(0))
+        self.own_done = True
+
     def finish(self):
         p = self.p
-        settle(self.source, self.own(0))
+        if not self.own_done:
+            self.settle_own()
         for k in range(p.n_hi):
 
             @pl.when(p.has_up & (p.hi >= k))
@@ -682,164 +688,265 @@
     return jax.ShapeDtypeStruct(dims, dtype)
 
 
-def opening_kernel(rows, seqs, x, g, wqkv, wgu, wdown, wout, gains, xs, gs, vqkv, vgu, vdown, vout, vgains, sems):
+def nt(left, right):
+    return lax.dot_general(left, right, (((1,), (1,)), ((), ())), preferred_element_type=jnp.float32)
+
+
+def tn(left, right):
+    return lax.dot_general(left, right, (((0,), (0,)), ((), ())), preferred_element_type=jnp.float32)
+
+
+def nn(left, right):
+    return lax.dot_general(left, right, (((1,), (0,)), ((), ())), preferred_element_type=jnp.float32)
+
+
+def rows_at(index, count):
+    return pl.ds(pl.multiple_of(index * count, count), count)
+
+
+def norm_rows(source, target, gain):
+    @pl.loop(0, source.shape[0] // 16)
+    def _(tile):
+        rows = rows_at(tile, 16)
+        values = source[rows, :].astype(jnp.float32)
+        target[rows, :] = rms_norm(values, gain[...]).astype(target.dtype)
+
+
+def attention(qkv, attended, key_place, query_low, query_high, shift, turned, head, head_size):
+    tokens, own_width = attended.shape
+    scale = head_size ** (-0.5)
+    keys_step = 256
+    lanes = pl.ds(head * head_size, head_size)
+    key_lanes = pl.ds(own_width + head * head_size, head_size)
+    value_lanes = pl.ds(2 * own_width + head * head_size, head_size)
+    turned[...] = jnp.zeros_like(turned)
+
+    @pl.loop(0, tokens // keys_step)
+    def _(step):
+        rows = rows_at(step, keys_step)
+        places = key_place[rows, :]
+        allowed = (places >= query_low[...]) & (places <= query_high[...])
+        scores = nt(qkv[rows, key_lanes], qkv[:, lanes]) * scale - shift[...]
+        sig = jnp.where(allowed, jax.nn.sigmoid(scores), 0.0).astype(jnp.bfloat16)
+        turned[...] += nn(qkv[rows, value_lanes].T, sig)
+
+    attended[:, lanes] = turned[...].T.astype(jnp.bfloat16)
+
+
+def forward_kernel(
+    rows,
+    seqs,
+    head_size,
+    x,
+    g,
+    wqkv,
+    wgu,
+    wdown,
+    wout,
+    gains,
+    key_place,
+    query_low,
+    query_high,
+    shift,
+    gs,
+    vgu,
+    vdown,
+    vout,
+    h2,
+    vqkv,
+    hn,
+    qkv,
+    attended,
+    middle,
+    gain_rows_out,
+    xs,
+    vgains,
+    heads,
+    turned,
+    out_held,
+    h2_own,
+    copies,
+    sems,
+):
     p, pool = Place(rows, seqs), Sems(sems)
     greet(p.peers() + p.rows())
-    half = x.shape[0] // 2
-    down_blocks, down_rows = vdown.shape[1], vdown.shape[2]
-
-    def part(source, target, c):
+    tokens, width = x.shape
+    half = tokens // 2
+    own_width = heads.shape[1]
+    deep = wout.shape[0]
+    down_blocks = vdown.shape[1]
+
+    def part(source, target, c, arrived=no_op):
         piece = pl.ds(c * half, half)
-        return SeqGather(p, pool, source.at[piece], lambda b: target.at[b, piece])
+        return SeqGather(p, pool, source.at[piece], lambda b: target.at[b, piece], arrived)
+
+    def norm_half(c):
+        def run(b):
+            start = pl.multiple_of(b * tokens + c * half, half)
+            norm_rows(xs.at[b, pl.ds(c * half, half)], hn.at[pl.ds(start, half), :], gain_rows_out.at[0:1, :])
+
+        return run
 
     qkv_rows = RowForward(p, pool, seqs, lambda r, b: vqkv.at[r, b])
     gu_rows = RowForward(p, pool, seqs, lambda r, b: vgu.at[r, b])
     down_fwd = RowForward(p, pool, down_blocks, lambda r, b: vdown.at[r, b])
     out_rows = RowForward(p, pool, seqs, lambda r, b: vout.at[r, b])
     gain_rows = RowForward(p, pool, seqs, lambda r, b: vgains.at[r, b])
-    x_parts = [part(x, xs, c) for c in range(2)]
+    x_parts = [part(x, xs, c, norm_half(c)) for c in range(2)]
     g_parts = [part(g, gs, c) for c in range(2)]
-    qkv = SeqExchange(p, pool, lambda t: wqkv.at[t], lambda b: vqkv.at[p.r, b], qkv_rows.forward)
-    gu = SeqExchange(p, pool, lambda t: wgu.at[t], lambda b: vgu.at[p.r, b], gu_rows.forward)
+    h2_parts = [part(h2_own, h2, c) for c in range(2)]
+    qkv_swap = SeqExchange(p, pool, lambda t: wqkv.at[t], lambda b: vqkv.at[p.r, b], qkv_rows.forward)
+    gu_swap = SeqExchange(p, pool, lambda t: wgu.at[t], lambda b: vgu.at[p.r, b], gu_rows.forward)
     out = SeqGather(p, pool, wout, lambda b: vout.at[p.r, b], out_rows.forward)
     gain = SeqGather(p, pool, gains, lambda b: vgains.at[p.r, b], gain_rows.forward)
+    heads_swap = SeqExchange(
+        p, pool, lambda t: heads.at[rows_at(t, tokens), :], lambda b: columns(attended, b, own_width)
+    )
     down_own = pool.take(1)
 
     gain.start()
     gain_rows.forward(p.s, gains)
-    qkv.start()
-    qkv_rows.forward(p.s, wqkv.at[p.s])
     for member in x_parts:
         member.start()
+    qkv_swap.start()
+    qkv_rows.forward(p.s, wqkv.at[p.s])
     pltpu.make_async_copy(wdown, vdown.at[p.r], down_own(0)).start()
     for block in range(down_blocks):
         down_fwd.forward(block, wdown.at[block])
+
+    for k in range(1, p.n_hi):
+        gain.step(k)
+    for k in range(p.n_hi):
+        gain.aside(k)
+    for block in range(seqs):
+        gain_rows.relay(block)
+    gain.finish()
+    gain_rows.finish()
+    for pair in range(rows * seqs // 2):
+        tile = vgains[2 * pair // seqs, 2 * pair % seqs] + vgains[2 * pair // seqs, 2 * pair % seqs + 1]
+        gain_rows_out[:, pl.ds(pair * 2 * deep, 2 * deep)] = tile
+
+    out_rows.forward(p.s, wout)
+    for c, member in enumerate(x_parts):
+        member.settle_own()
+        norm_half(c)(p.s)
+    for k in range(1, p.n_hi):
+        for member in x_parts:
+            member.step(k)
+        for step in (2 * k - 1, 2 * k):
+            qkv_swap.step(step)
+        if k == p.n_hi - 1:
+            out.start()
+    qkv_swap.step(seqs - 1)
     gu_rows.forward(p.s, wgu.at[p.s])
-    out_rows.forward(p.s, wout)
-    gu.start()
-    out.start()
+    for k in range(p.n_hi):
+        if k > 0:
+            out.step(k)
+        for member in x_parts:
+            member.aside(k)
+    gu_swap.start()
+    for block in range(seqs):
+        qkv_rows.relay(block)
+    qkv_swap.finish()
+    qkv_rows.finish()
+
+    weights = vqkv.reshape(width, 3 * own_width)
+
+    @pl.loop(0, seqs // 2)
+    def _(step):
+        tall = rows_at(step, 2 * tokens)
+        qkv[tall, :] = nn(hn[tall, :], weights[...]).astype(jnp.bfloat16)
+
+    for k in range(p.n_hi):
+        out.aside(k)
     for member in g_parts:
         member.start()
-    gathers = [gain] + x_parts + [out] + g_parts
+    own_heads = own_width // head_size
+    share = -(-seqs // own_heads)
+    for head in range(own_heads):
+        attention(qkv, heads, key_place, query_low, query_high, shift, turned, head, head_size)
+        for block in range(seqs)[head * share : (head + 1) * share]:
+            out_rows.relay(block)
+    heads_swap.start()
+    for step in range(1, seqs):
+        gu_swap.step(step)
+    out.finish()
+    out_rows.finish()
+    for r in range(rows):
+        pltpu.make_async_copy(vout.at[r], out_held.at[r], copies.at[r]).start()
+    for step in range(1, seqs):
+        heads_swap.step(step)
+    heads_swap.finish()
+    for r in range(rows):
+        settle(out_held.at[r], copies.at[r])
+    out_weights = out_held.reshape(width, width)
+    for member in g_parts:
+        member.step(1)
+
+    @pl.loop(0, width // 512)
+    def _(c):
+        lanes = rows_at(c, 512)
+        middle[:, lanes] = xs[p.s, :, lanes].astype(jnp.float32) + nn(attended[...], out_weights[:, lanes])
+
+    norm_rows(middle, h2_own, gain_rows_out.at[4:5, :])
+    for member in h2_parts:
+        member.start()
     for k in range(1, p.n_hi):
-        for member in gathers:
+        for member in h2_parts:
             member.step(k)
-        for step in (2 * k - 1, 2 * k):
-            qkv.step(step)
-            gu.step(step)
-    qkv.step(seqs - 1)
-    gu.step(seqs - 1)
+        if k > 1:
+            for member in g_parts:
+                member.step(k)
+    for block in range(down_blocks):
+        down_fwd.relay(block)
+    for block in range(seqs):
+        gu_rows.relay(block)
     for k in range(p.n_hi):
-        for member in gathers:
+        for member in h2_parts + g_parts:
             member.aside(k)
-    for member in (gain_rows, qkv_rows, down_fwd, gu_rows, out_rows):
-        for block in range(member.blocks):
-            member.relay(block)
-    for member in gathers + [qkv, gu, gain_rows, qkv_rows, down_fwd, gu_rows, out_rows]:
+    for member in x_parts + g_parts + h2_parts + [gu_swap, down_fwd, gu_rows]:
         member.finish()
-    settle(wdown, down_own(0))
-
-
-def opening(rows, seqs, x, g, wqkv, wgu, wdown, wout, gains):
+    settle(vdown.at[p.r], down_own(0))
+
+
+def forward(rows, seqs, head_size, x, g, wqkv, wgu, wdown, wout, gains, meta):
+    low, f32 = jnp.bfloat16, jnp.float32
     tokens, width = x.shape
     wdown = wdown.reshape(4, wdown.shape[0] // 4, width)
-    args = (x, g, wqkv, wgu, wdown, wout, gains)
+    own_width = width // seqs
+    row_tokens = tokens * seqs
     shapes = (
         shape_of((seqs, tokens, width)),
-        shape_of((seqs, tokens, width)),
-        shape_of((rows,) + wqkv.shape),
         shape_of((rows,) + wgu.shape),
         shape_of((rows,) + wdown.shape),
         shape_of((rows, seqs) + wout.shape),
-        shape_of((rows, seqs) + gains.shape, jnp.float32),
-    )
+        shape_of((seqs, tokens, width)),
+        shape_of((rows,) + wqkv.shape),
+        shape_of((row_tokens, width)),
+        shape_of((row_tokens, 3 * own_width)),
+        shape_of((tokens, width)),
+        shape_of((tokens, width), f32),
+        shape_of((8, width), f32),
+    )
+    scratch = [
+        pltpu.VMEM((seqs, tokens, width), low),
+        pltpu.VMEM((rows, seqs) + gains.shape, f32),
+        pltpu.VMEM((row_tokens, own_width), low),
+        pltpu.VMEM((head_size, row_tokens), f32),
+        pltpu.VMEM((rows, seqs) + wout.shape, low),
+        pltpu.VMEM((tokens, width), low),
+        pltpu.SemaphoreType.DMA((rows,)),
+    ]
     return call(
-        functools.partial(opening_kernel, rows, seqs), shapes, 1, args, [pl.ANY] * 7, (pl.ANY,) * 7, [], 640
-    )
-
-
-def spread_kernel(rows, seqs, source, target, sems):
-    p, pool = Place(rows, seqs), Sems(sems)
-    greet(p.chain())
-    half = source.shape[0] // 2
-    members = []
-    for c in range(2):
-        piece = pl.ds(c * half, half)
-        members.append(SeqGather(p, pool, source.at[piece], lambda b, piece=piece: target.at[b, piece]))
-    for member in members:
-        member.start()
-    for k in range(1, p.n_hi):
-        for member in members:
-            member.step(k)
-    for k in range(p.n_hi):
-        for member in members:
-            member.aside(k)
-    for member in members:
-        member.finish()
-
-
-def spread(rows, seqs, ident, source):
-    return call(
-        functools.partial(spread_kernel, rows, seqs),
-        shape_of((seqs,) + source.shape),
-        ident,
-        (source,),
-        [pltpu.VMEM],
-        pltpu.VMEM,
-        [],
-        128,
-    )
-
-
-def to_tokens_kernel(rows, seqs, source, target, sems):
-    p, pool = Place(rows, seqs), Sems(sems)
-    greet(p.peers())
-    width = source.shape[2]
-    member = SeqExchange(p, pool, lambda t: source.at[t], lambda b: columns(target, b, width))
-    member.start()
-    for step in range(1, seqs):
-        member.step(step)
-    member.finish()
-
-
-def to_heads_kernel(rows, seqs, source, target, sems):
-    p, pool = Place(rows, seqs), Sems(sems)
-    greet(p.peers())
-    width = target.shape[2]
-    member = SeqExchange(p, pool, lambda t: columns(source, t, width), lambda b: target.at[b])
-    member.start()
-    for step in range(1, seqs):
-        member.step(step)
-    member.finish()
-
-
-def to_tokens(rows, seqs, ident, source):
-    tokens = source.shape[0] // seqs
-    width = source.shape[1]
-    return call(
-        functools.partial(to_tokens_kernel, rows, seqs),
-        shape_of((tokens, width * seqs)),
-        ident,
-        (source.reshape(seqs, tokens, width),),
-        [pltpu.VMEM],
-        pltpu.VMEM,
-        [],
-        64,
-    )
-
-
-def to_heads(rows, seqs, ident, source):
-    tokens, width = source.shape[0], source.shape[1] // seqs
-    return call(
-        functools.partial(to_heads_kernel, rows, seqs),
-        shape_of((seqs, tokens, width)),
-        ident,
-        (source,),
-        [pltpu.VMEM],
-        pltpu.VMEM,
-        [],
-        64,
-    ).reshape(seqs * tokens, width)
+        functools.partial(forward_kernel, rows, seqs, head_size),
+        shapes,
+        1,
+        (x, g, wqkv, wgu, wdown, wout, gains) + meta,
+        [pl.ANY] * 7 + [pltpu.VMEM] * 4,
+        (pl.ANY,) * 5 + (pltpu.VMEM,) * 6,
+        scratch,
+        800,
+    )
 
 
 def seq_reducers(place, pool, source, side, chain, target):
@@ -992,18 +1099,6 @@
             settle(self.piece(p.s), self.recv(p.peer(step)))
 
 
-def nt(left, right):
-    return lax.dot_general(left, right, (((1,), (1,)), ((), ())), preferred_element_type=jnp.float32)
-
-
-def tn(left, right):
-    return lax.dot_general(left, right, (((0,), (0,)), ((), ())), preferred_element_type=jnp.float32)
-
-
-def nn(left, right):
-    return lax.dot_general(left, right, (((1,), (0,)), ((), ())), preferred_element_type=jnp.float32)
-
-
 def attention_back(qkv, do, dqkv, key_place, query_low, query_high, shift, dq_turned, head_size):
     tokens, own_width = do.shape
     scale = head_size ** (-0.5)
@@ -1271,10 +1366,8 @@
     deep = w_query.shape[0]
     row_tokens = tokens * seqs
     head_size = width // HEADS
-    scale = head_size ** (-0.5)
     own_width = width // seqs
     hidden_own = w_gate.shape[1] // seqs
-    heads_own = HEADS // seqs
     hidden_block = hidden_own // rows
 
     def by_heads(weight):
@@ -1287,42 +1380,42 @@
 
     wqkv = jnp.concatenate([by_heads(w_query), by_heads(w_key), by_heads(w_value)], axis=2)
     wgu = jnp.concatenate([by_hidden(w_gate), by_hidden(w_up)], axis=2)
-    gains_own = jnp.concatenate([gain_attn, gain_mlp]).astype(f32)[None, :]
-    gains_own = jnp.broadcast_to(gains_own, (8, 2 * deep))
+    side = lax.rem(lax.axis_index("seq"), 2)
+    lane = lax.broadcasted_iota(jnp.int32, (8, 2 * deep), 1)
+    both = [jnp.concatenate([gain, gain]).astype(f32)[None, :] for gain in (gain_attn, gain_mlp)]
+    number = lax.broadcasted_iota(jnp.int32, (8, 2 * deep), 0)
+    gains_own = jnp.where(lane // deep == side, jnp.where(number < 4, both[0], both[1]), 0.0)
     x_low, g_low = inputs[0], cotangent[0]
-    x_all, g_all, wqkv, wgu, wdown, wout, gains = opening(
-        rows, seqs, x_low, g_low, wqkv, wgu, w_down, w_out, gains_own
-    )
-    gains = gains[:, :, 0, :].reshape(rows * seqs, 2, deep)
-    gain_one, gain_two = gains[:, 0].reshape(width), gains[:, 1].reshape(width)
+
+    def places(shape, axis):
+        index = lax.broadcasted_iota(jnp.int32, shape, axis)
+        block, within = index // tokens, lax.rem(index, tokens)
+        segment = position = length_of = jnp.zeros_like(index)
+        begin = 0
+        for n in range(lengths.shape[1]):
+            unit = lengths[0, n] // (2 * seqs)
+            inside = (within >= begin) & (within < begin + 2 * unit)
+            local = within - begin
+            here = jnp.where(local < unit, block * unit + local, (2 * seqs - 1 - block) * unit + local - unit)
+            segment = jnp.where(inside, n, segment)
+            position = jnp.where(inside, here, position)
+            length_of = jnp.where(inside, lengths[0, n], length_of)
+            begin = begin + 2 * unit
+        return segment * row_tokens, segment * row_tokens + position, length_of
+
+    query_low, query_high, length_of = places((1, row_tokens), 1)
+    meta = (places((row_tokens, 1), 0)[1], query_low, query_high, jnp.log(length_of.astype(f32)))
+    g_all, wgu, wdown, wout, h2, wqkv, hn, qkv, attended, middle, gains = forward(
+        rows, seqs, head_size, x_low, g_low, wqkv, wgu, w_down, w_out, gains_own, meta
+    )
+    gain_one, gain_two = gains[0:1], gains[4:5]
     wqkv = wqkv.reshape(width, 3 * own_width)
     wgu = wgu.reshape(width, 2 * hidden_own)
     wdown = wdown.reshape(hidden_own, width)
     wout = wout.reshape(width, width)
     g_all = g_all.reshape(row_tokens, width)
-
-    x_full = x_all.reshape(row_tokens, width).astype(f32)
-    hn = rms_norm(x_full, gain_one).astype(low)
-    qkv = dot(hn, wqkv).astype(low)
-    queries, keys, values = (
-        qkv[:, n * own_width : (n + 1) * own_width].reshape(row_tokens, heads_own, head_size) for n in range(3)
-    )
-    meta = layout(lengths[0], jnp.arange(row_tokens, dtype=jnp.int32), tokens, seqs)
-    segment, position, length_of = meta
-    allowed = (segment[:, None] == segment[None, :]) & (position[None, :] <= position[:, None])
-    shift = jnp.log(length_of.astype(f32))[None, :, None]
-
-    def sigmoids():
-        scores = jnp.einsum("qhd,khd->hqk", queries, keys, preferred_element_type=f32) * scale
-        return jnp.where(allowed[None], jax.nn.sigmoid(scores - shift), 0.0)
-
-    sig_low = sigmoids().astype(low)
-    attended = jnp.einsum("hqk,khd->qhd", sig_low, values, preferred_element_type=f32)
-    attended = to_tokens(rows, seqs, 2, attended.reshape(row_tokens, own_width).astype(low))
-
+    h2 = h2.reshape(row_tokens, width)
     residual = x_low.astype(f32)
-    middle = residual + dot(attended, wout)
-    h2 = spread(rows, seqs, 3, rms_norm(middle, gain_two).astype(low)).reshape(row_tokens, width)
     gate_up = dot(h2, wgu)
     gate, up = gate_up[:, :hidden_own], gate_up[:, hidden_own:]
     gated, gated_back = jax.vjp(lambda a, b: jax.nn.silu(a) * b, gate, up)
@@ -1347,15 +1440,8 @@
     branch = middle_grad.astype(low)
     grad_out = dot(attended, branch, 0, 0).astype(low)
     do_own = dot(branch, wout, 1, 1).astype(low)
-    place = segment * row_tokens + position
-    back_meta = (
-        place[:, None],
-        (segment * row_tokens)[None, :],
-        place[None, :],
-        jnp.log(length_of.astype(f32))[None, :],
-    )
     hn_grad, sum_out, got_query, got_key, got_value, got_gate, got_up, got_gain = back(
-        rows, seqs, head_size, do_own, qkv, hn, wqkv, grad_out, sum_gu, gain_two_part, gain_one[None, :], back_meta
+        rows, seqs, head_size, do_own, qkv, hn, wqkv, grad_out, sum_gu, gain_two_part, gain_one, meta
     )
     spread_inverse = lax.rsqrt(jnp.mean(residual * residual, axis=-1, keepdims=True) + EPSILON)
     scaled_grad = gain_one * hn_grad

time: 650 us -> 616 us (0.948)
  Pallas kernels: 506 us -> 491 us
  matrix products: 85.2 us -> 77 us
    pallas_call x5 -> x3, Pallas kernels: 506 us -> 491 us  [call(): pl.pallas_call(kernel, out_shape=shapes, in_specs=[pl.BlockSpec(memory_sp...]
    dot_general x10 -> x8, matrix products: 80.1 us -> 77 us  [dot(): lax.dot_general(left, right, (((left_axis,), (right_axis,)), ((), ())), p...]
where the time goes in v4:
time: 616 us; the launch traced here: 611 us
  Pallas kernels  491 us (80%)
  matrix products  77 us (12%)
  other arithmetic  27.9 us (5%)
  local copies, waits for them, and re-layouts  8.43 us (1%)
  between operations  6.36 us (1%)
    pallas_call x3, Pallas kernels, call(): pl.pallas_call(kernel, out_shape=shapes, in_specs=[pl.BlockSpec(memory_sp...  491 us
    dot_general x8, matrix products, dot(): lax.dot_general(left, right, (((left_axis,), (right_axis,)), ((), ())), p...  77 us

profile of v4, /device:TPU:0, one launch (start us, length us, event | category | flops | bytes accessed | tf_op | source)
XLA Modules:
  0.0 611.1 jit_solution(1224327439619781171)
XLA Ops:
  0.7 1.3 fusion.44
  8.7 1.9 convert_log_fusion.shift
  18.5 1.5 pad_maximum_fusion.3.wgu
  20.0 241.8 %shard_map.203 = (bf16[8,128,2048]{2,1,0:T(8,128)(2,1)}, bf16[4,8,64,2048]{3,2,1,0:T(8,128)(2,1)}, bf16[4,4,64,2048]{3,2,1,0:T(8,128)(2,1)}, bf16[4,8,64,2048]{3...) custom-call(bf16[128,2048]{1,0:T(8,128)(2,1)} %bitcast.79, ...), custom_call_target="tpu_custom_call" | custom-call | tf_op jit(solution)/shard_map/pallas_call | solution.py:675
  261.8 1.5 fusion.43
  263.3 14.7 %fusion.45 = f32[1024,2048]{0,1:T(8,128)} fusion(bf16[1024,2048]{1,0:T(8,128)(2,1)} %bitcast.106, bf16[2048,2048]{1,0:T(8,128)(2,1)} %bitcast.100), kind=kOutput, calls=%fused_computation.106 | convolution fusion | flops 8589934592 | bytes 20971520 | tf_op jit(solution)/shard_map/dot_general | solution.py:1343
  278.0 10.5 %fusion.2 = (bf16[1024,1024]{0,1:T(8,128)(2,1)}, bf16[1024,1024]{0,1:T(8,128)(2,1)}, bf16[1024,1024]{0,1:T(8,128)(2,1)}) fusion(f32[1024,2048]{0,1:T(8,128)} %fusion.45, bf16[1024,2048]{1,0:T(8,128)(2,1)S(1)} %bitcast.104, bf16[1024,2048]{1,0:T(8,128)(2,1)S(1)} %bitcast.102), kind=kOutput, calls=%fused_computation.5 | convolution fusion | flops 4311744512 | bytes 23068672 | tf_op jit(solution)/shard_map/dot_general | solution.py:1343
  288.6 12.0 %convolution_convert_fusion.2 = bf16[1024,2048]{1,0:T(8,128)(2,1)} fusion(bf16[2048,2048]{1,0:T(8,128)(2,1)S(1)} %bitcast.101, bf16[1024,1024]{0,1:T(8,128)(2,1)} %get-tuple-element.62, bf16[1024,1024]{0,1:T(8,128)(2,1)} %get-tuple-element.61), kind=kOutput, calls=%fused_computation.11 | convolution fusion | flops 8600420352 | bytes 16777216 | tf_op jit(solution)/shard_map/dot_general | solution.py:1343
  300.6 14.6 %convolution_convert_fusion = bf16[2048,2048]{1,0:T(8,128)(2,1)} fusion(bf16[1024,2048]{1,0:T(8,128)(2,1)} %bitcast.107, bf16[1024,1024]{0,1:T(8,128)(2,1)} %get-tuple-element.62, bf16[1024,1024]{0,1:T(8,128)(2,1)} %get-tuple-element.61), kind=kOutput, calls=%fused_computation | convolution fusion | flops 8602517504 | bytes 16777216 | tf_op jit(solution)/shard_map/dot_general | solution.py:1343
  315.2 6.1 convolution_convert_fusion.3
  321.3 6.2 %convolution_convert_fusion.4 = bf16[1024,2048]{1,0:T(8,128)(2,1)} fusion(bf16[1024,1024]{0,1:T(8,128)(2,1)S(1)} %copy-done.19, bf16[1024,2048]{1,0:T(8,128)(2,1)S(1)} %bitcast.103), kind=kOutput, calls=%fused_computation.13 | convolution fusion | flops 4297064448 | bytes 10485760 | tf_op jit(solution)/shard_map/dot_general | solution.py:1343
  327.5 106.2 %shard_map.204 = (f32[128,2048]{1,0:T(8,128)}, f32[128,2048]{1,0:T(8,128)}, bf16[8,64,2048]{2,1,0:T(8,128)(2,1)}, bf16[4,64,2048]{2,1,0:T(8,128)(2,1)}) custom-call(bf16[8,128,2048]{2,1,0:T(8,128)(2,1)} %bitcast.80, bf16[8,128,2048]{2,1,0:T(8,128)(2,1)} %bitcast.82, bf16[4,8,64,2048]{3,2,1,0:T(8,128)(2,1)} %bitcast.78, bf16[4,4,64,2048]{3,2,1,0:T(8,128)(2,1)} %bitcast.81), custom_call_target="tpu_custom_call" | custom-call | tf_op jit(solution)/shard_map/pallas_call | solution.py:675
  433.7 1.6 multiply_reduce_fusion.1
  435.4 2.0 bitcast_reduce_fusion.gain_two_part
  438.6 7.2 %convolution_convert_fusion.5.do_own = bf16[128,2048]{1,0:T(8,128)(2,1)} fusion(bf16[2048,2048]{1,0:T(8,128)(2,1)} %bitcast.77, f32[128,2048]{1,0:T(8,128)S(1)} %get-tuple-element.64), kind=kOutput, calls=%fused_computation.14 | convolution fusion | flops 1074266112 | bytes 9961472 | tf_op jit(solution)/shard_map/dot_general | solution.py:1343
  445.8 1.6 bitcast_convert_fusion
  447.4 5.6 convolution_convert_fusion.1
  453.0 143.5 %shard_map.205 = (f32[128,2048]{1,0:T(8,128)}, bf16[64,2048]{1,0:T(8,128)(2,1)}, bf16[64,2048]{1,0:T(8,128)(2,1)}, bf16[64,2048]{1,0:T(8,128)(2,1)}, bf16[64,204...) custom-call(bf16[128,2048]{1,0:T(8,128)(2,1)} %convolution_convert_fusion.5.do_own, ...), custom_call_target="tpu_custom_call" | custom-call | tf_op jit(solution)/shard_map/pallas_call | solution.py:675
  596.6 1.6 fusion.4
  598.2 2.6 fusion.7
  601.5 1.8 convert_element_type.104
  603.3 1.8 convert_element_type.105
  606.7 2.7 convert_element_type.108
  609.4 1.5 convert_element_type.109
  (67 shorter events, 12.9 us)
Async XLA Ops:
  0.6 14.9 %copy-start.8 = (bf16[64,8192]{1,0:T(8,128)(2,1)S(1)}, bf16[64,8192]{1,0:T(8,128)(2,1)}, u32[]{:S(2)}) copy-start(bf16[64,8192]{1,0:T(8,128)(2,1)} %param.19) | copy-start | bytes 3145732
  14.6 2.4 copy-start.9
  263.3 14.7 %copy-start.16 = (bf16[4,4,64,2048]{3,2,1,0:T(8,128)(2,1)S(1)}, bf16[4,4,64,2048]{3,2,1,0:T(8,128)(2,1)}, u32[]{:S(2)}) copy-start(bf16[4,4,64,2048]{3,2,1,0:T(8,128)(2,1)} %get-tuple-element.36) | copy-start | bytes 12582916
  263.3 14.7 %copy-start.17 = (bf16[8,128,2048]{2,1,0:T(8,128)(2,1)S(1)}, bf16[8,128,2048]{2,1,0:T(8,128)(2,1)}, u32[]{:S(2)}) copy-start(bf16[8,128,2048]{2,1,0:T(8,128)(2,1)} %get-tuple-element.35) | copy-start | bytes 12582916
  278.0 10.6 %copy-start.15 = (bf16[4,8,64,2048]{3,2,1,0:T(8,128)(2,1)S(1)}, bf16[4,8,64,2048]{3,2,1,0:T(8,128)(2,1)}, u32[]{:S(2)}) copy-start(bf16[4,8,64,2048]{3,2,1,0:T(8,128)(2,1)} %get-tuple-element.38) | copy-start | bytes 25165828
  300.6 14.6 %copy-start.18 = (bf16[8,128,2048]{2,1,0:T(8,128)(2,1)S(1)}, bf16[8,128,2048]{2,1,0:T(8,128)(2,1)}, u32[]{:S(2)}) copy-start(bf16[8,128,2048]{2,1,0:T(8,128)(2,1)} %get-tuple-element.35) | copy-start | bytes 12582916
  300.6 14.6 %copy-start.19 = (bf16[1024,1024]{0,1:T(8,128)(2,1)S(1)}, bf16[1024,1024]{0,1:T(8,128)(2,1)}, u32[]{:S(2)}) copy-start(bf16[1024,1024]{0,1:T(8,128)(2,1)} %get-tuple-element.63) | copy-start | bytes 6291460
  327.5 106.2 %copy-start = (f32[128,2048]{1,0:T(8,128)S(1)}, f32[128,2048]{1,0:T(8,128)}, u32[]{:S(2)}) copy-start(f32[128,2048]{1,0:T(8,128)} %get-tuple-element.34) | copy-start | bytes 3145732
  433.7 3.7 copy-start.1
  433.7 3.7 copy-start.2
  433.7 3.7 copy-start.4
  433.7 3.7 copy-start.10
  438.6 7.2 %copy-start.7 = (bf16[4,64,2048]{2,1,0:T(8,128)(2,1)S(1)}, bf16[4,64,2048]{2,1,0:T(8,128)(2,1)}, u32[]{:S(2)}) copy-start(bf16[4,64,2048]{2,1,0:T(8,128)(2,1)} %get-tuple-element.56) | copy-start | bytes 3145732
  438.6 8.8 %copy-start.5 = (bf16[128,2048]{1,0:T(8,128)(2,1)S(1)}, bf16[128,2048]{1,0:T(8,128)(2,1)}, u32[]{:S(2)}) copy-start(bf16[128,2048]{1,0:T(8,128)(2,1)} %get-tuple-element.46) | copy-start | bytes 1572868
  453.0 143.6 %copy-start.3 = (bf16[1,128,2048]{2,1,0:T(8,128)(2,1)S(1)}, bf16[1,128,2048]{2,1,0:T(8,128)(2,1)}, u32[]{:S(2)}) copy-start(bf16[1,128,2048]{2,1,0:T(8,128)(2,1)} %param.12) | copy-start | bytes 1572868
  453.0 143.6 %copy-start.13 = (f32[1,2048]{1,0:T(1,128)S(1)}, f32[1,2048]{1,0:T(1,128)}, u32[]{:S(2)}) copy-start(f32[1,2048]{1,0:T(1,128)} %get-tuple-element.66.gain_one) | copy-start | bytes 24580
  596.6 4.3 copy-start.14
  596.6 8.5 %copy-start.12 = (bf16[64,2048]{1,0:T(8,128)(2,1)S(1)}, bf16[64,2048]{1,0:T(8,128)(2,1)}, u32[]{:S(2)}) copy-start(bf16[64,2048]{1,0:T(8,128)(2,1)} %get-tuple-element.51) | copy-start | bytes 786436
  596.6 9.3 %copy-start.11 = (bf16[64,2048]{1,0:T(8,128)(2,1)S(1)}, bf16[64,2048]{1,0:T(8,128)(2,1)}, u32[]{:S(2)}) copy-start(bf16[64,2048]{1,0:T(8,128)(2,1)} %get-tuple-element.52) | copy-start | bytes 786436
  598.2 11.2 %copy-start.6 = (bf16[64,8192]{1,0:T(8,128)(2,1)S(1)}, bf16[64,8192]{1,0:T(8,128)(2,1)}, u32[]{:S(2)}) copy-start(bf16[64,8192]{1,0:T(8,128)(2,1)} %get-tuple-element.55) | copy-start | bytes 3145732
